TPU v7x, 128 devices: a whole 4x4x4 slice. The times are simulated.
128 devices in a mesh: dp: 16 (over x, z), tensor: 8 (over y, core).
Axes of the slice: x: 4, y: 4, z: 4, core: 2. Of those that a mesh axis runs over, the one named last changes fastest.
Arguments:
- embeddings: bfloat16 [8192, 2048], P('dp', 'tensor'), may hold values from -6 to 6
- trunk_weights: bfloat16 [2, 2048, 2048], P(None, None, 'tensor'), may hold values from -0.125 to 0.125
- trunk_gains: float32 [2, 2048], replicated, may hold values from 0.1 to 1.9
- expert_weights: bfloat16 [8, 2048, 2048], P('tensor'), may hold values from -0.125 to 0.125
- route_ids: int32 [8192, 2], P('dp'), may hold values from 0 to 7, all different within a row; in each aligned block of 512 rows (0 to 511, 512 to 1023, ...) at most 256 rows name the same one
- task_gates: float32 [8192, 2, 2], P('dp'), may hold values from 0.2 to 1
- mixture_grad: bfloat16 [2, 8192, 2048], P(None, 'dp', 'tensor'), may hold values from -0.119628906 to 0.119628906
Outputs:
- task_mixture: bfloat16 [2, 8192, 2048], P(None, 'dp', 'tensor')
- expert_grad: float32 [8, 2048, 2048], P('tensor', 'dp')
Inputs may be any that keep to these rules, and one draw needn't show every extreme that they name: `route_ids`: the 2 experts of an example differ. In each aligned block of 512 examples (the examples of one index of dp) no expert is chosen more than 256 times, and some expert is chosen exactly 256 times in some block.
All inputs are finite; a program needn't handle non-finite values.
Results may differ from a plain program's by a relative error of at most 0.014.
Values may be sent and summed in bfloat16 or wider, within the bound.
A program may use at most 128 MiB of HBM per device.

v0:
```python
import math

import jax
import jax.numpy as jnp
from jax import lax
from jax.sharding import PartitionSpec as P

NEMB = 16
DEMB = 128


def silu_grad(pre_act):
    sigma = jax.nn.sigmoid(pre_act)
    return sigma + pre_act * sigma * (1.0 - sigma)


def slot_tables(route_block, experts, capacity):
    flat_ids = route_block.reshape(-1)
    count = flat_ids.shape[0]
    onehot = (flat_ids[:, None] == jnp.arange(experts, dtype=jnp.int32)[None, :]).astype(jnp.int32)
    running = jnp.cumsum(onehot, axis=0) - 1
    place = jnp.sum(onehot * running, axis=1)
    slot_index = flat_ids * capacity + place
    slot_source = (
        jnp.full((experts * capacity,), count, jnp.int32)
        .at[slot_index]
        .set(jnp.arange(count, dtype=jnp.int32))
    )
    return (slot_index, slot_source)


def interaction(whole, gain):
    wide = whole.astype(jnp.float32)
    scale = lax.rsqrt(jnp.mean(wide * wide, axis=1, keepdims=True) + 1e-05)
    normed = (wide * scale * gain[None, :]).astype(jnp.bfloat16)
    cube = normed.reshape(normed.shape[0], NEMB, DEMB)
    gram = jnp.einsum("rnd,rmd->rnm", cube, cube, preferred_element_type=jnp.float32) / math.sqrt(
        DEMB
    )
    inter = jnp.einsum(
        "rnm,rmd->rnd", gram, cube.astype(jnp.float32), precision=lax.Precision.HIGHEST
    ) / math.sqrt(NEMB)
    return inter.reshape(whole.shape[0], NEMB * DEMB).astype(jnp.bfloat16)


def on_device(
    embeddings, trunk_weights, trunk_gains, expert_weights, route_ids, task_gates, mixture_grad
):
    trunk = embeddings
    for block_index in range(trunk_weights.shape[0]):
        whole = lax.all_gather(trunk, "tensor", axis=1, tiled=True)
        inter = interaction(whole, trunk_gains[block_index])
        branch = jax.nn.silu(
            jnp.dot(inter, trunk_weights[block_index], preferred_element_type=jnp.float32)
        )
        trunk = (trunk.astype(jnp.float32) + branch).astype(jnp.bfloat16)
    experts = lax.axis_size("tensor")
    local_rows, top_count = route_ids.shape
    count = local_rows * top_count
    capacity = 2 * count // experts
    slot_index, slot_source = slot_tables(route_ids, experts, capacity)
    source_rows = slot_source // top_count
    padded = jnp.concatenate([trunk, jnp.zeros((1, trunk.shape[1]), jnp.bfloat16)], axis=0)
    outgoing = padded[source_rows].reshape(experts, capacity, trunk.shape[1])
    expert_rows = lax.all_to_all(outgoing, "tensor", split_axis=0, concat_axis=2, tiled=True)[0]
    pre_act = jnp.dot(expert_rows, expert_weights[0], preferred_element_type=jnp.float32)
    outputs = jax.nn.silu(pre_act).astype(jnp.bfloat16)
    returned = lax.all_to_all(outputs[None], "tensor", split_axis=2, concat_axis=0, tiled=True)
    hidden_share = returned.shape[2]
    picked = returned.reshape(experts * capacity, hidden_share)[slot_index].reshape(
        local_rows, top_count, hidden_share
    )
    mixture = jnp.sum(task_gates[:, :, :, None] * picked[:, None, :, :].astype(jnp.float32), axis=2)
    task_mixture = jnp.transpose(mixture, (1, 0, 2)).astype(jnp.bfloat16)
    out_grad = jnp.einsum("rtk,trh->rkh", task_gates, mixture_grad.astype(jnp.float32)).astype(
        jnp.bfloat16
    )
    grad_pad = jnp.concatenate(
        [out_grad.reshape(count, hidden_share), jnp.zeros((1, hidden_share), jnp.bfloat16)], axis=0
    )
    outgoing_grad = grad_pad[slot_source].reshape(experts, capacity, hidden_share)
    slot_grad = lax.all_to_all(outgoing_grad, "tensor", split_axis=0, concat_axis=2, tiled=True)[0]
    pre_grad = (slot_grad.astype(jnp.float32) * silu_grad(pre_act)).astype(jnp.bfloat16)
    row_share = expert_rows.shape[1] // lax.axis_size("dp")
    local_grad = lax.dot_general(
        expert_rows, pre_grad, (((0,), (0,)), ((), ())), preferred_element_type=jnp.float32
    )
    summed = lax.psum(local_grad, "dp")
    weight_grad = lax.dynamic_slice_in_dim(summed, lax.axis_index("dp") * row_share, row_share, 0)
    return (task_mixture, weight_grad[None])


def solution(mesh):
    in_specs = (
        P("dp", "tensor"),
        P(None, None, "tensor"),
        P(),
        P("tensor", None, None),
        P("dp", None),
        P("dp", None, None),
        P(None, "dp", "tensor"),
    )
    out_specs = (P(None, "dp", "tensor"), P("tensor", "dp", None))
    return jax.shard_map(
        on_device, mesh=mesh, in_specs=in_specs, out_specs=out_specs, check_vma=False
    )
```

profile of v0, /device:TPU:1, one launch (start us, length us, event | category | flops | bytes accessed | tf_op | source)
XLA Modules:
  0.0 362.3 jit_solution(12338588220182082461)
XLA Ops:
  8.8 31.8 %all-gather.3.cloned.1.call-done = bf16[512,2048]{1,0:T(8,128)(2,1)} async-done(((bf16[512,256]{1,0:T(8,128)(2,1)}), bf16[512,2048]{1,0:T(8,128)(2,1)}) %all-gather.3.cloned.1.call-update) | async-done | bytes 2097168 | tf_op jit(solution)/shard_map/all_gather | solution.py:51
  40.6 2.2 fusion.2
  44.1 1.2 fusion.58
  45.4 2.7 multiply_convert_fusion.1
  48.1 1.4 add_convert_fusion.1
  50.4 2.3 reduce-window.6
  54.6 4.3 %scatter_custom_fusion = s32[2048]{0:T(1024)S(1)} fusion(s32[1024]{0:T(1024)S(1)} %bitcast.112, s32[1024]{0:T(1024)S(1)} %iota.11, s32[]{:T(128)} %constant.56.clone.1), kind=kCustom, calls=%fused_computation.71 | custom fusion | bytes 8196 | tf_op jit(solution)/shard_map/scatter | solution.py:27
  58.9 9.0 %gather_fusion.2 = bf16[2048,256]{1,0:T(8,128)(2,1)} fusion(bf16[1025,256]{1,0:T(8,128)(2,1)S(1)} %concatenate.7, s32[2048]{0:T(1024)S(1)} %get-tuple-element.4), kind=kCustom, calls=%fused_computation.2 | custom fusion | bytes 2105344 | tf_op jit(solution)/shard_map/gather | solution.py:81
  67.9 4.2 %all-to-all-start.2 = ((bf16[8,256,256]{2,1,0:T(8,128)(2,1)}), bf16[8,256,256]{2,1,0:T(8,128)(2,1)S(1)}, u32[]{:S(2)}, u32[]{:S(2)}) async-start(bf16[8,256,256]{2,1,0:T(8,128)(2,1)} %bitcast.104), calls=%async_computation.2 | async-start | bytes 2097152 | tf_op jit(solution)/shard_map/all_to_all | solution.py:82
  72.2 8.1 %all-gather.5.cloned.1.call-done = bf16[512,2048]{1,0:T(8,128)(2,1)} async-done(((bf16[512,256]{1,0:T(8,128)(2,1)}), bf16[512,2048]{1,0:T(8,128)(2,1)}) %all-gather.5.cloned.1.call-update) | async-done | bytes 2097168 | tf_op jit(solution)/shard_map/all_gather | solution.py:51
  80.3 2.2 fusion.5
  83.8 1.2 fusion.59
  85.0 2.7 multiply_convert_fusion
  88.5 7.5 %gather_fusion = bf16[2048,256]{1,0:T(8,128)(2,1)S(1)} fusion(bf16[513,256]{1,0:T(8,128)(2,1)S(1)} %concatenate.6, s32[2048]{0:T(1024)S(1)} %get-tuple-element.5), kind=kCustom, calls=%fused_computation | custom fusion | bytes 2105344 | tf_op jit(solution)/shard_map/gather | solution.py:64
  96.0 1.3 copy.46
  97.4 5.4 %all-to-all-start = ((bf16[8,256,256]{1,2,0:T(8,128)(2,1)}), bf16[8,256,256]{1,2,0:T(8,128)(2,1)S(1)}, u32[]{:S(2)}, u32[]{:S(2)}) async-start(bf16[8,256,256]{1,2,0:T(8,128)(2,1)} %copy.46), calls=%async_computation | async-start | bytes 2097152 | tf_op jit(solution)/shard_map/all_to_all | solution.py:65
  103.0 1.6 copy.59
  104.6 13.3 %all-to-all-done = bf16[8,256,256]{1,2,0:T(8,128)(2,1)S(1)} async-done(((bf16[8,256,256]{1,2,0:T(8,128)(2,1)}), bf16[8,256,256]{1,2,0:T(8,128)(2,1)S(1)}, u32[]{:S(2)}, u32[]{:S(2)}) %all-to-all-start) | async-done | bytes 1048608 | tf_op jit(solution)/shard_map/all_to_all | solution.py:65
  118.9 6.2 %fusion = f32[256,2048]{1,0:T(8,128)S(1)} fusion(bf16[256,2048]{0,1:T(8,128)(2,1)} %bitcast.98, bf16[1,2048,2048]{2,1,0:T(8,128)(2,1)} %param.10), kind=kOutput, calls=%fused_computation.4 | convolution fusion | flops 2147483648 | bytes 11534336 | tf_op jit(solution)/shard_map/dot_general | solution.py:66
  125.1 8.3 %fusion.28 = f32[2048,2048]{1,0:T(8,128)} fusion(bf16[256,2048]{0,1:T(8,128)(2,1)S(1)} %bitcast.99, f32[256,2048]{1,0:T(8,128)S(1)} %bitcast.102, f32[256,2048]{1,0:T(8,128)S(1)} %fusion), kind=kOutput, calls=%fused_computation.39 | convolution fusion | flops 2152202240 | bytes 22020096 | tf_op jit(solution)/shard_map/dot_general | solution.py:85
  133.4 1.5 fusion.34
  134.9 4.6 %copy.47 = bf16[1,256,2048]{1,0,2:T(2,128)(2,1)S(1)} copy(bf16[1,256,2048]{2,1,0:T(8,128)(2,1)} %fusion.34) | data formatting | bytes 2097152 | tf_op jit(solution)/shard_map/broadcast_in_dim | solution.py:68
  140.0 11.6 %reduce.2 = bf16[2048,256]{1,0:T(8,128)(2,1)} reduce(bf16[2048,1,256]{2,1,0:T(2,128)(2,1)S(1)} %bitcast.101, bf16[]{:T(256)} %broadcast.160), dimensions={1}, to_apply=%bitcast.76.reduce_sub_computation | reduce | bytes 2097154
  151.6 2.2 reshape.154
  153.8 5.0 %all-to-all-start.1 = ((bf16[8,2,32768]{2,1,0:T(2,128)(2,1)}), bf16[8,2,32768]{2,1,0:T(2,128)(2,1)}, u32[]{:S(2)}, u32[]{:S(2)}) async-start(bf16[8,2,32768]{2,1,0:T(2,128)(2,1)} %reshape.154), calls=%async_computation.1 | async-start | bytes 2097152 | tf_op jit(solution)/shard_map/all_to_all | solution.py:68
  158.8 15.2 %all-to-all-done.1 = bf16[8,2,32768]{2,1,0:T(2,128)(2,1)} async-done(((bf16[8,2,32768]{2,1,0:T(2,128)(2,1)}), bf16[8,2,32768]{2,1,0:T(2,128)(2,1)}, u32[]{:S(2)}, u32[]{:S(2)}) %all-to-all-start.1) | async-done | bytes 1048608 | tf_op jit(solution)/shard_map/all_to_all | solution.py:68
  174.0 4.3 %reshape.155 = bf16[2048,1,256]{2,1,0:T(2,128)(2,1)S(1)} reshape(bf16[8,2,32768]{2,1,0:T(2,128)(2,1)} %all-to-all-done.1) | data formatting | bytes 2097152
  179.5 1.5 copy.48
  181.0 3.9 %gather_fusion.1 = bf16[1024,256]{1,0:T(8,128)(2,1)S(1)} fusion(bf16[2048,256]{1,0:T(8,128)(2,1)S(1)} %bitcast.97, s32[1024]{0:T(1024)S(1)} %broadcast_clamp_fusion), kind=kCustom, calls=%fused_computation.1 | custom fusion | bytes 1052672 | tf_op jit(solution)/shard_map/gather | solution.py:70
  185.5 1.2 multiply_reduce_fusion
  186.7 166.8 %all-reduce.4.cloned.1.call-done = f32[2048,2048]{1,0:T(8,128)} async-done(((f32[2048,2048]{1,0:T(8,128)}), f32[2048,2048]{1,0:T(8,128)}) %all-reduce.4.cloned.1.call-update) | async-done | bytes 16777232 | tf_op jit(solution)/shard_map/psum | solution.py:88
  353.5 2.3 dynamic-slice_bitcast_fusion
  (66 shorter events, 10.9 us)
Async XLA Ops:
  7.2 46.3 %copy-start = (bf16[2,512,256]{2,1,0:T(8,128)(2,1)S(1)}, bf16[2,512,256]{2,1,0:T(8,128)(2,1)}, u32[]{:S(2)}) copy-start(bf16[2,512,256]{2,1,0:T(8,128)(2,1)} %param.13) | copy-start | bytes 1572868
  7.2 33.4 %all-gather.3.cloned.1.call-start = ((), (), s32[]{:S(2)}) async-start(), calls=%async_computation.3 | async-start | bytes 2359296 | tf_op jit(solution)/shard_map/all_gather | solution.py:51
  7.9 72.4 %all-gather.5.cloned.1.call-start = ((), (), s32[]{:S(2)}) async-start(), calls=%async_computation.4 | async-start | bytes 2359296 | tf_op jit(solution)/shard_map/all_gather | solution.py:51
  40.6 2.2 copy-start.5
  45.3 2.7 copy-start.7
  45.3 2.7 copy-start.11
  48.1 1.5 copy-start.10
  48.1 5.1 %copy-start.9 = (f32[512,2,2]{0,2,1:T(2,128)S(1)}, f32[512,2,2]{0,2,1:T(2,128)}, u32[]{:S(2)}) copy-start(f32[512,2,2]{0,2,1:T(2,128)} %param.12) | copy-start | bytes 24580
  67.9 29.4 %all-to-all-start.2 = ((bf16[8,256,256]{2,1,0:T(8,128)(2,1)}), bf16[8,256,256]{2,1,0:T(8,128)(2,1)S(1)}, u32[]{:S(2)}, u32[]{:S(2)}) async-start(bf16[8,256,256]{2,1,0:T(8,128)(2,1)} %bitcast.104), calls=%async_computation.2 | async-start | bytes 2097152 | tf_op jit(solution)/shard_map/all_to_all | solution.py:82
  80.3 2.2 copy-start.4
  85.0 2.7 copy-start.8
  85.0 2.7 copy-start.12
  97.4 20.5 %all-to-all-start = ((bf16[8,256,256]{1,2,0:T(8,128)(2,1)}), bf16[8,256,256]{1,2,0:T(8,128)(2,1)S(1)}, u32[]{:S(2)}, u32[]{:S(2)}) async-start(bf16[8,256,256]{1,2,0:T(8,128)(2,1)} %copy.46), calls=%async_computation | async-start | bytes 2097152 | tf_op jit(solution)/shard_map/all_to_all | solution.py:65
  102.8 250.7 %all-reduce.4.cloned.1.call-start = ((), (), s32[]{:S(2)}) async-start(), calls=%async_computation.5 | async-start | bytes 33554432 | tf_op jit(solution)/shard_map/psum | solution.py:88
  117.9 1.0 copy-start.2
  118.9 6.2 %copy-start.3 = (bf16[8,256,256]{1,2,0:T(8,128)(2,1)S(1)}, bf16[8,256,256]{1,2,0:T(8,128)(2,1)}, u32[]{:S(2)}) copy-start(bf16[8,256,256]{1,2,0:T(8,128)(2,1)} %copy-done.2) | copy-start | bytes 3145732
  118.9 6.2 %copy-start.6 = (f32[32,8,8,256]{3,1,2,0:T(8,128)S(1)}, f32[32,8,8,256]{3,1,2,0:T(8,128)}, u32[]{:S(2)}) copy-start(f32[32,8,8,256]{3,1,2,0:T(8,128)} %copy.59) | copy-start | bytes 6291460
  153.8 20.2 %all-to-all-start.1 = ((bf16[8,2,32768]{2,1,0:T(2,128)(2,1)}), bf16[8,2,32768]{2,1,0:T(2,128)(2,1)}, u32[]{:S(2)}, u32[]{:S(2)}) async-start(bf16[8,2,32768]{2,1,0:T(2,128)(2,1)} %reshape.154), calls=%async_computation.1 | async-start | bytes 2097152 | tf_op jit(solution)/shard_map/all_to_all | solution.py:68
  185.5 170.3 %copy-start.1 = (bf16[2,512,256]{2,1,0:T(8,128)(2,1)S(1)}, bf16[2,512,256]{2,1,0:T(8,128)(2,1)}, u32[]{:S(2)}) copy-start(bf16[2,512,256]{2,1,0:T(8,128)(2,1)} %param.13) | copy-start | bytes 1572868
Sparse Core Ops, SparseCore 0:
  9.7 30.8 all-gather.2
  49.7 30.5 all-gather.4
  133.5 219.9 all-reduce.3
where the time goes:
time: 363 us; the launch traced here: 362 us
  waiting for transfers between devices  236 us (65%)
  local copies, waits for them, and re-layouts  49.5 us (14%)
  matrix products  25.2 us (7%)
  other arithmetic  22.7 us (6%)
  starting transfers between devices  14.8 us (4%)
  between operations  14.1 us (4%)
    psum x1, waiting for transfers between devices, on_device(): summed = lax.psum(local_grad, 'dp')  167 us
    all_gather x2, waiting for transfers between devices, on_device(): whole = lax.all_gather(trunk, 'tensor', axis=1, tiled=True)  40 us
    all_to_all x1, waiting for transfers between devices, on_device(): lax.all_to_all(outputs[None], 'tensor', split_axis=2, concat_axis=0, tile...  15.2 us
    all_to_all x1, waiting for transfers between devices, on_device(): lax.all_to_all(outgoing, 'tensor', split_axis=0, concat_axis=2, tiled=True)  13.3 us
    unnamed x5, other arithmetic  13 us
    unnamed x35, local copies, waits for them, and re-layouts  12.4 us
    gather x1, local copies, waits for them, and re-layouts, on_device(): grad_pad[slot_source].reshape(experts, capacity, hidden_share)  9.01 us
    dot_general x1, matrix products, on_device(): lax.dot_general(expert_rows, pre_grad, (((0,), (0,)), ((), ())), preferre...  8.27 us
  transfers between devices with their start and end apart: 6, of which 5 were waited for; matrix products, arithmetic and copies ran while one was open for 20% of the time, Pallas kernels for 0%

commit v1 on v0

v1 whole, which is shorter than its diff:
```python
import math

import jax
import jax.numpy as jnp
from jax import lax
from jax.sharding import PartitionSpec as P

NEMB = 16
DEMB = 128
F32 = jnp.float32
BF16 = jnp.bfloat16


def silu_grad(pre_act):
    sigma = jax.nn.sigmoid(pre_act)
    return sigma + pre_act * sigma * (1.0 - sigma)


def slot_table(route, experts, capacity):
    rows = route.shape[0]
    lanes = jnp.arange(experts, dtype=jnp.int32)
    member = jnp.sum((route[:, :, None] == lanes).astype(F32), axis=1)
    earlier = (jnp.arange(rows)[:, None] > jnp.arange(rows)[None, :]).astype(BF16)
    prefix = jnp.dot(earlier, member.astype(BF16), preferred_element_type=F32).astype(jnp.int32)
    place = jnp.sum((route[:, :, None] == lanes) * prefix[:, None, :], axis=2)
    return route * capacity + place


def interaction(whole, gain):
    wide = whole.astype(F32)
    scale = lax.rsqrt(jnp.mean(wide * wide, axis=1, keepdims=True) + 1e-05)
    normed = (wide * scale * gain[None, :]).astype(BF16)
    cube = normed.reshape(normed.shape[0], NEMB, DEMB)
    gram = jnp.einsum("rnd,rmd->rnm", cube, cube, preferred_element_type=F32) / math.sqrt(DEMB)
    inter = jnp.einsum(
        "rnm,rmd->rnd", gram, cube.astype(F32), precision=lax.Precision.HIGHEST
    ) / math.sqrt(NEMB)
    return inter.reshape(whole.shape[0], NEMB * DEMB).astype(BF16)


def on_device(
    embeddings, trunk_weights, trunk_gains, expert_weights, route_ids, task_gates, mixture_grad
):
    trunk = embeddings
    for block_index in range(trunk_weights.shape[0]):
        whole = lax.all_gather(trunk, "tensor", axis=1, tiled=True)
        inter = interaction(whole, trunk_gains[block_index])
        branch = jax.nn.silu(
            jnp.dot(inter, trunk_weights[block_index], preferred_element_type=F32)
        )
        trunk = (trunk.astype(F32) + branch).astype(BF16)
    experts = lax.axis_size("tensor")
    local_rows, top_count = route_ids.shape
    capacity = 2 * local_rows * top_count // experts
    width = trunk.shape[1]
    slots = slot_table(route_ids, experts, capacity)
    all_slots = jnp.arange(experts * capacity, dtype=jnp.int32)
    hot = [(slots[:, k][None, :] == all_slots[:, None]).astype(BF16) for k in range(top_count)]
    outgoing = jnp.dot(sum(hot), trunk, preferred_element_type=F32).astype(BF16)
    expert_rows = lax.all_to_all(
        outgoing.reshape(experts, capacity, width), "tensor", split_axis=0, concat_axis=2, tiled=True
    )[0]
    wide_grad = mixture_grad.astype(F32)
    sent_grad = 0.0
    for k in range(top_count):
        out_grad = (
            task_gates[:, 0, k, None] * wide_grad[0] + task_gates[:, 1, k, None] * wide_grad[1]
        ).astype(BF16)
        sent_grad = sent_grad + jnp.dot(hot[k], out_grad, preferred_element_type=F32)
    slot_grad = lax.all_to_all(
        sent_grad.astype(BF16).reshape(experts, capacity, width),
        "tensor", split_axis=0, concat_axis=2, tiled=True,
    )[0]
    pre_act = jnp.dot(expert_rows, expert_weights[0], preferred_element_type=F32)
    outputs = jax.nn.silu(pre_act).astype(BF16)
    pre_grad = (slot_grad.astype(F32) * silu_grad(pre_act)).astype(BF16)
    local_grad = lax.dot_general(
        expert_rows, pre_grad, (((0,), (0,)), ((), ())), preferred_element_type=F32
    ).astype(BF16)
    weight_grad = lax.psum_scatter(local_grad, "dp", scatter_dimension=0, tiled=True).astype(F32)
    returned = lax.all_to_all(
        outputs.reshape(capacity, experts, width).transpose(1, 0, 2),
        "tensor", split_axis=0, concat_axis=0, tiled=True,
    ).reshape(experts * capacity, width)
    mixture = 0.0
    for k in range(top_count):
        picked = lax.dot_general(
            hot[k], returned, (((0,), (0,)), ((), ())), preferred_element_type=F32
        )
        mixture = mixture + task_gates[:, :, k].T[:, :, None] * picked[None]
    return (mixture.astype(BF16), weight_grad[None])


def solution(mesh):
    in_specs = (
        P("dp", "tensor"),
        P(None, None, "tensor"),
        P(),
        P("tensor", None, None),
        P("dp", None),
        P("dp", None, None),
        P(None, "dp", "tensor"),
    )
    out_specs = (P(None, "dp", "tensor"), P("tensor", "dp", None))
    return jax.shard_map(
        on_device, mesh=mesh, in_specs=in_specs, out_specs=out_specs, check_vma=False
    )
```

time: 363 us -> 224 us (0.62)
  waiting for transfers between devices: 236 us -> 147 us
  local copies, waits for them, and re-layouts: 49.5 us -> 7.08 us
  other arithmetic: 22.7 us -> 9.26 us
  matrix products: 25.2 us -> 32.4 us
    psum x1 -> x0, waiting for transfers between devices: 167 us -> none  [on_device(): summed = lax.psum(local_grad, 'dp')]
    reduce_scatter x0 -> x1, waiting for transfers between devices: none -> 58.3 us  [on_device(): lax.psum_scatter(local_grad, 'dp', scatter_dimension=0, tiled=True)]
    gather x3 -> x0, local copies, waits for them, and re-layouts: 20.4 us -> none  [the longest x1 9.01 us: on_device(): grad_pad[slot_source].reshape(experts, capacity, hidden_share)]
    all_gather x2, waiting for transfers between devices: 40 us -> 58.6 us  [on_device(): whole = lax.all_gather(trunk, 'tensor', axis=1, tiled=True)]
    unnamed x5 -> x3, other arithmetic: 13 us -> 1.4 us
    dot_general x8 -> x12, matrix products: 17 us -> 26.7 us  [the longest x1 7.01 us: on_device(): jnp.dot(expert_rows, expert_weights[0], preferred_element_type=F32)]
    unnamed x35 -> x21, local copies, waits for them, and re-layouts: 12.4 us -> 2.94 us
    broadcast_in_dim x2 -> x0, local copies, waits for them, and re-layouts: 6.89 us -> none  [the longest x1 4.6 us: on_device(): outputs[None]]
  transfers between devices with their start and end apart: 6 -> 6, of which waited for: 5 -> 5; matrix products, arithmetic and copies ran while one was open for 20% -> 11% of each run, Pallas kernels for 0% -> 0%
where the time goes in v1:
time: 224 us; the launch traced here: 223 us
  waiting for transfers between devices  147 us (66%)
  matrix products  32.4 us (14%)
  between operations  14 us (6%)
  starting transfers between devices  13 us (6%)
  other arithmetic  9.26 us (4%)
  local copies, waits for them, and re-layouts  7.08 us (3%)
    all_gather x2, waiting for transfers between devices, on_device(): whole = lax.all_gather(trunk, 'tensor', axis=1, tiled=True)  58.6 us
    reduce_scatter x1, waiting for transfers between devices, on_device(): lax.psum_scatter(local_grad, 'dp', scatter_dimension=0, tiled=True)  58.3 us
    all_to_all x1, waiting for transfers between devices, on_device(): lax.all_to_all(outputs.reshape(capacity, experts, width).transpose(1, 0,...  15.1 us
    all_to_all x1, waiting for transfers between devices, on_device(): lax.all_to_all(outgoing.reshape(experts, capacity, width), 'tensor', spli...  14.7 us
    dot_general x1, matrix products, on_device(): jnp.dot(expert_rows, expert_weights[0], preferred_element_type=F32)  7.01 us
    dot_general x1, matrix products, on_device(): lax.dot_general(expert_rows, pre_grad, (((0,), (0,)), ((), ())), preferre...  5.75 us
    dot_general x2, matrix products, interaction(): jnp.einsum('rnm,rmd->rnd', gram, cube.astype(F32), precision=lax.Precisio...  5.39 us
    dot_general x1, matrix products, on_device(): outgoing = jnp.dot(sum(hot), trunk, preferred_element_type=F32).astype(BF16)  4.65 us
  transfers between devices with their start and end apart: 6, of which 5 were waited for; matrix products, arithmetic and copies ran while one was open for 11% of the time, Pallas kernels for 0%

profile of v1, /device:TPU:1, one launch (start us, length us, event | category | flops | bytes accessed | tf_op | source)
XLA Modules:
  0.0 223.0 jit_solution(2013557583025811274)
XLA Ops:
  7.2 0.7 all-gather.3.cloned.1.call-update
  7.9 0.8 fusion.73
  8.8 31.8 %all-gather.3.cloned.1.call-done = bf16[512,2048]{1,0:T(8,128)(2,1)} async-done(((bf16[512,256]{1,0:T(8,128)(2,1)}), bf16[512,2048]{1,0:T(8,128)(2,1)}) %all-gather.3.cloned.1.call-update) | async-done | bytes 2097168 | tf_op jit(solution)/shard_map/all_gather | solution.py:46
  40.6 2.2 fusion.2
  42.8 0.6 fusion.24
  43.5 0.6 copy.28
  44.1 1.2 fusion.78
  45.3 2.7 %multiply_convert_fusion.1 = bf16[512,16,128]{2,1,0:T(8,128)(2,1)S(1)} fusion(bf16[512,16,128]{2,1,0:T(8,128)(2,1)S(1)} %bitcast.113, f32[512,16,16]{2,1,0:T(8,128)S(1)} %fusion.78), kind=kOutput, calls=%fused_computation.16 | convolution fusion | flops 203554816 | bytes 4718592 | tf_op jit(solution)/shard_map/rnm,rmd->rnd/dot_general | solution.py:35
  48.1 1.4 add_convert_fusion.4
  50.2 0.9 fusion.12
  51.2 2.0 fusion.19
  53.2 4.2 %all-to-all-start.2 = ((bf16[8,256,256]{2,1,0:T(8,128)(2,1)}), bf16[8,256,256]{2,1,0:T(8,128)(2,1)S(1)}, u32[]{:S(2)}, u32[]{:S(2)}) async-start(bf16[8,256,256]{2,1,0:T(8,128)(2,1)} %bitcast.23), calls=%async_computation.2 | async-start | bytes 2097152 | tf_op jit(solution)/shard_map/all_to_all | solution.py:70
  57.4 26.7 %all-gather.5.cloned.1.call-done = bf16[512,2048]{1,0:T(8,128)(2,1)} async-done(((bf16[512,256]{1,0:T(8,128)(2,1)}), bf16[512,2048]{1,0:T(8,128)(2,1)}) %all-gather.5.cloned.1.call-update) | async-done | bytes 2097168 | tf_op jit(solution)/shard_map/all_gather | solution.py:46
  84.2 2.2 fusion.5
  87.0 0.6 copy.30
  87.6 1.2 fusion.79
  88.9 2.7 %multiply_convert_fusion = bf16[512,16,128]{2,1,0:T(8,128)(2,1)S(1)} fusion(bf16[512,16,128]{2,1,0:T(8,128)(2,1)S(1)} %bitcast.115, f32[512,16,16]{2,1,0:T(8,128)S(1)} %fusion.79), kind=kOutput, calls=%fused_computation.13 | convolution fusion | flops 203554816 | bytes 4718592 | tf_op jit(solution)/shard_map/rnm,rmd->rnd/dot_general | solution.py:35
  91.6 4.7 %convolution_convert_fusion.1 = bf16[2048,256]{1,0:T(8,128)(2,1)} fusion(s32[512]{0:T(512)S(1)} %bitcast.131, s32[512]{0:T(512)S(1)} %bitcast.128, bf16[2,2048,256]{2,1,0:T(8,128)(2,1)} %param.8, bf16[64,8,16,128]{3,2,1,0:T(8,128)(2,1)S(1)} %bitcast.117, bf16[512,256]{1,0:T(8,128)(2,1)S(1)} %copy-done.5), kind=kOutput, calls=%fused_computation.29 | convolution fusion | flops 1083572224 | bytes 4460544 | tf_op jit(solution)/shard_map/dot_general | solution.py:59
  96.2 2.3 %copy.22 = bf16[8,256,256]{1,2,0:T(8,128)(2,1)} copy(bf16[8,256,256]{2,1,0:T(8,128)(2,1)} %bitcast.124) | data formatting | bytes 2097152 | tf_op jit(solution)/shard_map/reshape | solution.py:61
  98.5 4.3 %all-to-all-start = ((bf16[8,256,256]{1,2,0:T(8,128)(2,1)}), bf16[8,256,256]{1,2,0:T(8,128)(2,1)S(1)}, u32[]{:S(2)}, u32[]{:S(2)}) async-start(bf16[8,256,256]{1,2,0:T(8,128)(2,1)} %copy.22), calls=%async_computation | async-start | bytes 2097152 | tf_op jit(solution)/shard_map/all_to_all | solution.py:60
  103.3 14.7 %all-to-all-done = bf16[8,256,256]{1,2,0:T(8,128)(2,1)S(1)} async-done(((bf16[8,256,256]{1,2,0:T(8,128)(2,1)}), bf16[8,256,256]{1,2,0:T(8,128)(2,1)S(1)}, u32[]{:S(2)}, u32[]{:S(2)}) %all-to-all-start) | async-done | bytes 1048608 | tf_op jit(solution)/shard_map/all_to_all | solution.py:60
  118.0 7.0 %fusion.44 = (bf16[256,2048]{1,0:T(8,128)(2,1)}, f32[256,2048]{1,0:T(8,128)S(1)}) fusion(bf16[256,2048]{0,1:T(8,128)(2,1)S(1)} %bitcast.121, bf16[1,2048,2048]{2,1,0:T(8,128)(2,1)} %param.10), kind=kOutput, calls=%fused_computation.51 | convolution fusion | flops 2150105088 | bytes 12582912 | tf_op jit(solution)/shard_map/dot_general | solution.py:74
  125.0 5.8 %convolution_convert_fusion = bf16[2048,2048]{1,0:T(8,128)(2,1)} fusion(bf16[256,2048]{0,1:T(8,128)(2,1)S(1)} %bitcast.122, f32[256,2048]{1,0:T(8,128)S(1)} %bitcast.116, f32[256,2048]{1,0:T(8,128)S(1)} %get-tuple-element.13), kind=kOutput, calls=%fused_computation.2 | convolution fusion | flops 2156396544 | bytes 13631488 | tf_op jit(solution)/shard_map/dot_general | solution.py:77
  130.7 1.2 copy-done.2
  131.9 1.0 copy.51
  133.0 4.3 %all-to-all-start.1 = ((bf16[8,256,256]{2,1,0:T(8,128)(2,1)}), bf16[8,256,256]{2,1,0:T(8,128)(2,1)S(1)}, u32[]{:S(2)}, u32[]{:S(2)}) async-start(bf16[8,256,256]{2,1,0:T(8,128)(2,1)} %bitcast.111), calls=%async_computation.1 | async-start | bytes 2097152 | tf_op jit(solution)/shard_map/all_to_all | solution.py:81
  137.3 15.1 %all-to-all-done.1 = bf16[8,256,256]{2,1,0:T(8,128)(2,1)S(1)} async-done(((bf16[8,256,256]{2,1,0:T(8,128)(2,1)}), bf16[8,256,256]{2,1,0:T(8,128)(2,1)S(1)}, u32[]{:S(2)}, u32[]{:S(2)}) %all-to-all-start.1) | async-done | bytes 1048608 | tf_op jit(solution)/shard_map/all_to_all | solution.py:81
  152.4 1.3 fusion.13
  153.7 1.3 fusion.16
  155.0 1.1 add_convert_fusion
  156.1 58.3 %reduce-scatter.2.cloned.1.call-done = bf16[128,2048]{1,0:T(8,128)(2,1)} async-done(((bf16[2048,2048]{1,0:T(8,128)(2,1)}), bf16[128,2048]{1,0:T(8,128)(2,1)}) %reduce-scatter.2.cloned.1.call-update) | async-done | bytes 524304 | tf_op jit(solution)/shard_map/reduce_scatter | solution.py:80
  214.4 2.1 bitcast_convert_fusion
  (37 shorter events, 1.8 us)
Async XLA Ops:
  7.2 33.4 %all-gather.3.cloned.1.call-start = ((), (), s32[]{:S(2)}) async-start(), calls=%async_computation.4 | async-start | bytes 2359296 | tf_op jit(solution)/shard_map/all_gather | solution.py:46
  7.9 76.3 %all-gather.5.cloned.1.call-start = ((), (), s32[]{:S(2)}) async-start(), calls=%async_computation.5 | async-start | bytes 2359296 | tf_op jit(solution)/shard_map/all_gather | solution.py:46
  40.6 2.2 %copy-start.1 = (bf16[512,2048]{1,0:T(8,128)(2,1)S(1)}, bf16[512,2048]{1,0:T(8,128)(2,1)}, u32[]{:S(2)}) copy-start(bf16[512,2048]{1,0:T(8,128)(2,1)} %all-gather.3.cloned.1.call-done) | copy-start | bytes 6291460
  45.3 2.7 %copy-start.4 = (bf16[512,256]{1,0:T(8,128)(2,1)S(1)}, bf16[512,256]{1,0:T(8,128)(2,1)}, u32[]{:S(2)}) copy-start(bf16[512,256]{1,0:T(8,128)(2,1)} %param.7) | copy-start | bytes 786436
  45.3 2.7 %copy-start.8 = (bf16[2,2048,256]{2,1,0:T(8,128)(2,1)S(1)}, bf16[2,2048,256]{2,1,0:T(8,128)(2,1)}, u32[]{:S(2)}) copy-start(bf16[2,2048,256]{2,1,0:T(8,128)(2,1)} %param.8) | copy-start | bytes 6291460
  48.1 1.5 copy-start.3
  48.1 1.6 copy-start.6
  49.5 0.7 copy-start.7
  53.2 45.3 %all-to-all-start.2 = ((bf16[8,256,256]{2,1,0:T(8,128)(2,1)}), bf16[8,256,256]{2,1,0:T(8,128)(2,1)S(1)}, u32[]{:S(2)}, u32[]{:S(2)}) async-start(bf16[8,256,256]{2,1,0:T(8,128)(2,1)} %bitcast.23), calls=%async_computation.2 | async-start | bytes 2097152 | tf_op jit(solution)/shard_map/all_to_all | solution.py:70
  84.2 2.2 %copy-start = (bf16[512,2048]{1,0:T(8,128)(2,1)S(1)}, bf16[512,2048]{1,0:T(8,128)(2,1)}, u32[]{:S(2)}) copy-start(bf16[512,2048]{1,0:T(8,128)(2,1)} %all-gather.5.cloned.1.call-done) | copy-start | bytes 6291460
  88.9 2.7 %copy-start.5 = (bf16[512,256]{1,0:T(8,128)(2,1)S(1)}, bf16[512,256]{1,0:T(8,128)(2,1)}, u32[]{:S(2)}) copy-start(bf16[512,256]{1,0:T(8,128)(2,1)} %add_convert_fusion.4) | copy-start | bytes 786436
  98.5 19.4 %all-to-all-start = ((bf16[8,256,256]{1,2,0:T(8,128)(2,1)}), bf16[8,256,256]{1,2,0:T(8,128)(2,1)S(1)}, u32[]{:S(2)}, u32[]{:S(2)}) async-start(bf16[8,256,256]{1,2,0:T(8,128)(2,1)} %copy.22), calls=%async_computation | async-start | bytes 2097152 | tf_op jit(solution)/shard_map/all_to_all | solution.py:60
  102.9 111.5 %reduce-scatter.2.cloned.1.call-start = ((), (), s32[]{:S(2)}) async-start(), calls=%async_computation.6 | async-start | bytes 8912896 | tf_op jit(solution)/shard_map/reduce_scatter | solution.py:80
  130.7 1.2 copy-start.2
  133.0 19.4 %all-to-all-start.1 = ((bf16[8,256,256]{2,1,0:T(8,128)(2,1)}), bf16[8,256,256]{2,1,0:T(8,128)(2,1)S(1)}, u32[]{:S(2)}, u32[]{:S(2)}) async-start(bf16[8,256,256]{2,1,0:T(8,128)(2,1)} %bitcast.111), calls=%async_computation.1 | async-start | bytes 2097152 | tf_op jit(solution)/shard_map/all_to_all | solution.py:81
Sparse Core Ops, SparseCore 0:
  9.7 30.8 all-gather.2
  49.7 34.4 all-gather.4
  130.9 83.4 reduce-scatter.1

commit v2 on v1

v2 whole, which is shorter than its diff:
```python
import math

import jax
import jax.numpy as jnp
from jax import lax
from jax.experimental import pallas as pl
from jax.experimental.pallas import tpu as pltpu
from jax.sharding import PartitionSpec as P

NEMB = 16
DEMB = 128
GROUP = 16
CHUNKS = 4
F32 = jnp.float32
BF16 = jnp.bfloat16
MESH = pl.DeviceIdType.MESH


def slot_table(route, experts, capacity):
    rows = route.shape[0]
    lanes = jnp.arange(experts, dtype=jnp.int32)
    member = jnp.sum((route[:, :, None] == lanes).astype(F32), axis=1)
    earlier = (jnp.arange(rows)[:, None] > jnp.arange(rows)[None, :]).astype(BF16)
    prefix = jnp.dot(earlier, member.astype(BF16), preferred_element_type=F32).astype(jnp.int32)
    place = jnp.sum((route[:, :, None] == lanes) * prefix[:, None, :], axis=2)
    return route * capacity + place


def dot(a, b):
    return jnp.dot(a, b, preferred_element_type=F32)


def remote(src, dst, send_sem, recv_sem, axis, index):
    return pltpu.make_async_remote_copy(
        src_ref=src, dst_ref=dst, send_sem=send_sem, recv_sem=recv_sem,
        device_id={axis: index}, device_id_type=MESH,
    )


def greet(axis_peers):
    barrier = pltpu.get_barrier_semaphore()
    for axis, peer in axis_peers:
        pl.semaphore_signal(barrier, inc=1, device_id={axis: peer}, device_id_type=MESH)
    pl.semaphore_wait(barrier, len(axis_peers))


def trunk_kernel(
    emb, gains, weights, slot_rows, gates, grad, rows_out, grad_out,
    whole, nrm, inter, mask, cot, outg, send, recv, gsend, grecv,
):
    n_dev, rows, width = outg.shape[0], emb.shape[0], emb.shape[1]
    step_rows = rows // CHUNKS
    half = step_rows // 2
    cap = outg.shape[1]
    ring = n_dev // 2
    me = lax.axis_index("tensor")
    y, core = me // 2, me % 2
    right = ((y + 1) % ring) * 2 + core
    left = ((y + ring - 1) % ring) * 2 + core
    far = ((y + 2) % ring) * 2 + core
    sib = y * 2 + 1 - core

    def block(i, owner, lo=0, size=step_rows):
        return whole.at[i // CHUNKS, owner, pl.ds((i % CHUNKS) * step_rows + lo, size)]

    def copy(i, which):
        owner, lo, size, to = (
            (me, 0, step_rows, sib), (me, 0, step_rows, right), (me, 0, step_rows, left),
            (left, 0, step_rows, sib), (right, 0, step_rows, sib),
            (left, half, half, right), (right, 0, half, left),
            (far, half, half, sib), (far, 0, half, sib),
        )[which]
        ref = block(i, owner, lo, size)
        return remote(ref, ref, send.at[i, which], recv.at[i, which], "tensor", to)

    sib_left, sib_right = left + 1 - 2 * core, right + 1 - 2 * core
    sib_far = far + 1 - 2 * core

    def arrived(i, which):
        owner, lo, size = (
            (sib, 0, step_rows), (left, 0, step_rows), (right, 0, step_rows),
            (sib_left, 0, step_rows), (sib_right, 0, step_rows),
            (far, half, half), (far, 0, half),
            (sib_far, half, half), (sib_far, 0, half),
        )[which]
        ref = block(i, owner, lo, size)
        remote(ref, ref, send.at[i, which], recv.at[i, which], "tensor", sib).wait_recv()

    def begin(i):
        for which in (1, 2, 0):
            copy(i, which).start()

    def relay(i):
        arrived(i, 1)
        copy(i, 5).start()
        arrived(i, 2)
        copy(i, 6).start()
        copy(i, 3).start()
        copy(i, 4).start()

    def relay_far(i):
        arrived(i, 5)
        copy(i, 7).start()
        arrived(i, 6)
        copy(i, 8).start()

    def complete(i):
        for which in (0, 3, 4, 7, 8):
            arrived(i, which)

    whole[0, me] = emb[...]
    greet([("tensor", (me + d) % n_dev) for d in range(1, n_dev)])

    @pl.loop(0, CHUNKS)
    def _(i):
        begin(i)

    row_id = lax.broadcasted_iota(jnp.int32, mask.shape, 0) % GROUP
    col_id = lax.broadcasted_iota(jnp.int32, mask.shape, 1) % GROUP
    mask[...] = jnp.where(row_id == col_id, 1.0 / math.sqrt(DEMB * NEMB), 0.0)
    relay(0)
    for k in range(2):
        cot[k] = (
            gates[:, k : k + 1] * grad[0].astype(F32) + gates[:, 2 + k : 3 + k] * grad[1].astype(F32)
        ).astype(BF16)
    relay(1)
    relay_far(0)

    def chosen(expert, k):
        wanted = lax.broadcasted_iota(jnp.int32, (cap, rows), 0) + expert * cap
        return (slot_rows[k : k + 1, :] == wanted).astype(F32).astype(BF16)

    @pl.loop(0, n_dev)
    def _(e):
        outg[e] = (dot(chosen(e, 0), cot[0]) + dot(chosen(e, 1), cot[1])).astype(BF16)

    def grad_copy(d):
        to = (me + d) % n_dev
        return remote(outg.at[to], grad_out.at[me], gsend.at[d], grecv.at[d], "tensor", to)

    grad_out[me] = outg[me]

    @pl.loop(0, 2 * CHUNKS)
    def _(i):
        stage, first = i // CHUNKS, (i % CHUNKS) * step_rows
        span = pl.ds(first, step_rows)
        relay(i + 2)
        relay_far(i + 1)
        complete(i)

        def tile(n):
            return whole[stage, n // 2, span, (n % 2) * DEMB : (n % 2 + 1) * DEMB].astype(F32)

        total = jnp.zeros((step_rows, DEMB), F32)
        for n in range(NEMB):
            x = tile(n)
            total = total + x * x
        mean = jnp.sum(total, axis=1, keepdims=True) / (NEMB * DEMB)
        scale = lax.rsqrt(mean + 1e-05)
        for n in range(NEMB):
            gain = gains[stage, :, n * DEMB : (n + 1) * DEMB]
            nrm[n] = (tile(n) * scale * gain).astype(BF16)

        @pl.loop(0, step_rows // GROUP // 4)
        def _(g4):
            for g in range(4):
                at = pl.ds(pl.multiple_of((g4 * 4 + g) * GROUP, GROUP), GROUP)
                stack = nrm[:, at, :].reshape(NEMB * GROUP, DEMB)
                gram = lax.dot_general(
                    stack, stack, (((1,), (1,)), ((), ())), preferred_element_type=F32
                ) * mask[...]
                high = gram.astype(BF16)
                low = (gram - high.astype(F32)).astype(BF16)
                mixed = (dot(high, stack) + dot(low, stack)).astype(BF16)
                mixed = mixed.reshape(NEMB, GROUP, DEMB)
                for n in range(NEMB):
                    inter[at, n * DEMB : (n + 1) * DEMB] = mixed[n]

        pre = dot(inter[...], weights[stage])
        value = whole[stage, me, span].astype(F32) + pre * jax.nn.sigmoid(pre)
        whole[stage + 1, me, span] = value.astype(BF16)
        begin(i + CHUNKS)

        @pl.when(i < n_dev - 1)
        def _():
            grad_copy(i + 1).start()

    for i in range(2 * CHUNKS, 3 * CHUNKS):
        if i + 2 < 3 * CHUNKS:
            relay(i + 2)
        if i + 1 < 3 * CHUNKS:
            relay_far(i + 1)
        complete(i)

    mine = (chosen(me, 0).astype(F32) + chosen(me, 1).astype(F32)).astype(BF16)
    for q in range(n_dev):
        rows_out[:, q * width : (q + 1) * width] = dot(mine, whole[2, q]).astype(BF16)

    @pl.loop(0, 3 * CHUNKS)
    def _(i):
        for which in range(9):
            copy(i, which).wait_send()

    @pl.loop(1, n_dev)
    def _(d):
        grad_copy(d).wait_send()
        source = (me + n_dev - d) % n_dev
        remote(
            outg.at[me], grad_out.at[source], gsend.at[d], grecv.at[d], "tensor", source
        ).wait_recv()


def expert_kernel(
    rows_in, weight, slot_grad, slot_cols, gates, mix_out, wgrad_out,
    held_weight, rows_t, pgrad, outs, ret, first_buf, ring_buf, last_buf,
    wsem, send1, recv1, send2, recv2, osend, orecv,
):
    n_dev, cap, width = outs.shape
    part = pgrad.shape[1] // 4
    piece = wgrad_out.shape[0]
    me = lax.axis_index("tensor")
    dp = lax.axis_index("dp")
    cx, cz = dp // 4, dp % 4

    def load(h):
        span = pl.ds(h * part, part)
        return pltpu.make_async_copy(weight.at[:, span], held_weight.at[:, span], wsem.at[h])

    for h in range(4):
        load(h).start()

    def place(h, u, v):
        return u * 4 + v if h < 2 else v * 4 + u

    coord = [(cx, cz), (cx, cz), (cz, cx), (cz, cx)]
    sign = [1, 3, 1, 3]

    greet(
        [("dp", place(0, (cx + 1) % 4, cz)), ("dp", place(0, (cx + 3) % 4, cz)),
         ("dp", place(0, cx, (cz + 1) % 4)), ("dp", place(0, cx, (cz + 3) % 4))]
        + [("tensor", (me + d) % n_dev) for d in range(1, n_dev)]
    )

    eye = (
        lax.broadcasted_iota(jnp.int32, (width, width), 0)
        == lax.broadcasted_iota(jnp.int32, (width, width), 1)
    ).astype(F32).astype(BF16)
    for q in range(n_dev):
        rows_t[q * width : (q + 1) * width, :] = lax.dot_general(
            eye, rows_in[:, q * width : (q + 1) * width], (((1,), (1,)), ((), ())),
            preferred_element_type=F32,
        ).astype(BF16)

    def partial(h, t, j):
        u, v = coord[h]
        owner = place(h, (u + (4 - sign[h]) * (1 + t)) % 4, (v + (4 - sign[h]) * (1 + j)) % 4)
        at = pl.ds(pl.multiple_of(owner * piece, piece), piece)
        return dot(rows_t[at, :], pgrad[:, h * part : (h + 1) * part])

    def hop1(h, k, src):
        u, v = coord[h]
        return remote(
            src, ring_buf.at[h, k], send1.at[h, k], recv1.at[h, k],
            "dp", place(h, (u + sign[h]) % 4, v),
        )

    def hop2(h, j):
        u, v = coord[h]
        return remote(
            ring_buf.at[h, 8 + j], last_buf.at[h, j], send2.at[h, j], recv2.at[h, j],
            "dp", place(h, u, (v + sign[h]) % 4),
        )

    for h in range(4):
        load(h).wait()
        for p in range(2 * h, 2 * h + 2):
            cols = slice(p * width, (p + 1) * width)
            pre = dot(rows_in[...], held_weight[:, cols])
            sigma = jax.nn.sigmoid(pre)
            outs[p] = (pre * sigma).astype(BF16)
            slope = sigma + pre * sigma * (1.0 - sigma)
            pgrad[:, cols] = (slot_grad[p].astype(F32) * slope).astype(BF16)

        @pl.loop(0, 4)
        def _(j):
            first_buf[h, j] = partial(h, 0, j).astype(BF16)
            hop1(h, j, first_buf.at[h, j]).start()

    def out_copy(d):
        to = (me + d) % n_dev
        return remote(outs.at[to], ret.at[me], osend.at[d], orecv.at[d], "tensor", to)

    @pl.loop(1, n_dev)
    def _(d):
        out_copy(d).start()

    ret[me] = outs[me]

    def ring_step(k):
        t, j = k // 4, k % 4
        for h in range(4):
            own = partial(h, t, j)
            hop1(h, k - 4, ring_buf.at[h, k - 4]).wait_recv()
            ring_buf[h, k - 4] = (ring_buf[h, k - 4].astype(F32) + own).astype(BF16)
            hop1(h, k, ring_buf.at[h, k - 4]).start()

    pl.loop(4, 8)(ring_step)

    @pl.loop(1, n_dev)
    def _(d):
        source = (me + n_dev - d) % n_dev
        remote(
            outs.at[me], ret.at[source], osend.at[d], orecv.at[d], "tensor", source
        ).wait_recv()

    block_rows = 128

    @pl.loop(0, mix_out.shape[1] // block_rows)
    def _(b):
        at = pl.ds(pl.multiple_of(b * block_rows, block_rows), block_rows)
        lane = lax.broadcasted_iota(jnp.int32, (block_rows, cap), 1)
        picked = []
        for k in range(2):
            slot = slot_cols[at, k : k + 1]
            total = jnp.zeros((block_rows, width), F32)
            for e in range(n_dev):
                hot = (slot == lane + e * cap).astype(F32).astype(BF16)
                total = total + dot(hot, ret[e])
            picked.append(total)
        for t in range(2):
            mix = (
                gates[at, 2 * t : 2 * t + 1] * picked[0]
                + gates[at, 2 * t + 1 : 2 * t + 2] * picked[1]
            )
            mix_out[t, at, :] = mix.astype(BF16)

    pl.loop(8, 12)(ring_step)

    for j in range(4):
        for h in range(4):
            own = partial(h, 3, j)
            hop1(h, 8 + j, ring_buf.at[h, 8 + j]).wait_recv()
            total = ring_buf[h, 8 + j].astype(F32) + own
            if j > 0:
                hop2(h, j - 1).wait_recv()
                total = total + last_buf[h, j - 1].astype(F32)
            if j < 3:
                ring_buf[h, 8 + j] = total.astype(BF16)
                hop2(h, j).start()
            else:
                wgrad_out[:, h * part : (h + 1) * part] = total

    for h in range(4):
        @pl.loop(0, 4)
        def _(k):
            hop1(h, k, first_buf.at[h, k]).wait_send()

        @pl.loop(4, 12)
        def _(k):
            hop1(h, k, ring_buf.at[h, k - 4]).wait_send()

        for j in range(3):
            hop2(h, j).wait_send()

    @pl.loop(1, n_dev)
    def _(d):
        out_copy(d).wait_send()


VMEM = pl.BlockSpec(memory_space=pltpu.VMEM)
DMA = pltpu.SemaphoreType.DMA


def on_device(
    embeddings, trunk_weights, trunk_gains, expert_weights, route_ids, task_gates, mixture_grad
):
    experts = lax.axis_size("tensor")
    rows, top = route_ids.shape
    cap = 2 * rows * top // experts
    width = embeddings.shape[1]
    full = width * experts
    slots = slot_table(route_ids, experts, cap)
    gates = task_gates.reshape(rows, -1)
    step_rows = rows // CHUNKS

    expert_rows, slot_grad = pl.pallas_call(
        trunk_kernel,
        out_shape=(
            jax.ShapeDtypeStruct((cap, full), BF16),
            jax.ShapeDtypeStruct((experts, cap, width), BF16),
        ),
        in_specs=[VMEM] * 6,
        out_specs=(VMEM, VMEM),
        scratch_shapes=[
            pltpu.VMEM((3, experts, rows, width), BF16),
            pltpu.VMEM((NEMB, step_rows, DEMB), BF16),
            pltpu.VMEM((step_rows, full), BF16),
            pltpu.VMEM((NEMB * GROUP, NEMB * GROUP), F32),
            pltpu.VMEM((2, rows, width), BF16),
            pltpu.VMEM((experts, cap, width), BF16),
            DMA((3 * CHUNKS, 9)),
            DMA((3 * CHUNKS, 9)),
            DMA((experts,)),
            DMA((experts,)),
        ],
        compiler_params=pltpu.CompilerParams(
            collective_id=0, has_side_effects=True, vmem_limit_bytes=40 << 20
        ),
        cost_estimate=pl.CostEstimate(flops=6 << 30, bytes_accessed=8 << 20, transcendentals=0),
        name="trunk",
    )(embeddings, trunk_gains[:, None, :], trunk_weights, slots.T, gates, mixture_grad)

    piece = full // lax.axis_size("dp")
    part = full // 4
    mixture, weight_grad = pl.pallas_call(
        expert_kernel,
        out_shape=(
            jax.ShapeDtypeStruct((2, rows, width), BF16),
            jax.ShapeDtypeStruct((piece, full), F32),
        ),
        in_specs=[VMEM, pl.BlockSpec(memory_space=pl.ANY), VMEM, VMEM, VMEM],
        out_specs=(VMEM, VMEM),
        scratch_shapes=[
            pltpu.VMEM((full, full), BF16),
            pltpu.VMEM((full, cap), BF16),
            pltpu.VMEM((cap, full), BF16),
            pltpu.VMEM((experts, cap, width), BF16),
            pltpu.VMEM((experts, cap, width), BF16),
            pltpu.VMEM((4, 4, piece, part), BF16),
            pltpu.VMEM((4, 12, piece, part), BF16),
            pltpu.VMEM((4, 3, piece, part), BF16),
            DMA((4,)),
            DMA((4, 12)),
            DMA((4, 12)),
            DMA((4, 3)),
            DMA((4, 3)),
            DMA((experts,)),
            DMA((experts,)),
        ],
        compiler_params=pltpu.CompilerParams(
            collective_id=1, has_side_effects=True, vmem_limit_bytes=48 << 20
        ),
        cost_estimate=pl.CostEstimate(flops=6 << 30, bytes_accessed=12 << 20, transcendentals=0),
        name="experts",
    )(expert_rows, expert_weights[0], slot_grad, slots, gates)
    return (mixture, weight_grad[None])


def solution(mesh):
    in_specs = (
        P("dp", "tensor"),
        P(None, None, "tensor"),
        P(),
        P("tensor", None, None),
        P("dp", None),
        P("dp", None, None),
        P(None, "dp", "tensor"),
    )
    out_specs = (P(None, "dp", "tensor"), P("tensor", "dp", None))
    return jax.shard_map(
        on_device, mesh=mesh, in_specs=in_specs, out_specs=out_specs, check_vma=False
    )
```

time: 224 us -> 134 us (0.60)
  waiting for transfers between devices: 147 us -> 0 us
  Pallas kernels: 0 us -> 122 us
  matrix products: 32.4 us -> 0.22 us
  between operations: 14 us -> 0.68 us
  starting transfers between devices: 13 us -> 0 us
  other arithmetic: 9.26 us -> 2.13 us
    pallas_call x0 -> x2, Pallas kernels: none -> 122 us  [the longest x1 61.2 us: on_device(): pl.pallas_call(trunk_kernel, out_shape=(jax.ShapeDtypeStruct((cap, full),...]
    all_gather x2 -> x0, waiting for transfers between devices: 58.6 us -> none  [on_device(): whole = lax.all_gather(trunk, 'tensor', axis=1, tiled=True)]
    reduce_scatter x1 -> x0, waiting for transfers between devices: 58.3 us -> none  [on_device(): lax.psum_scatter(local_grad, 'dp', scatter_dimension=0, tiled=True)]
    dot_general x12 -> x0, matrix products: 32.2 us -> none  [the longest x1 7.01 us: on_device(): jnp.dot(expert_rows, expert_weights[0], preferred_element_type=F32)]
    all_to_all x3 -> x0, waiting for transfers between devices: 29.8 us -> none  [the longest x1 15.1 us: on_device(): lax.all_to_all(outputs.reshape(capacity, experts, width).transpose(1, 0,...]
    all_to_all x3 -> x0, starting transfers between devices: 12.9 us -> none  [the longest x1 4.35 us: on_device(): lax.all_to_all(outgoing.reshape(experts, capacity, width), 'tensor', spli...]
    reduce_sum x2 -> x0, other arithmetic: 4.45 us -> none  [interaction(): scale = lax.rsqrt(jnp.mean(wide * wide, axis=1, keepdims=True) + 1e-05)]
    reshape x2, local copies, waits for them, and re-layouts: 3.3 us -> 0.86 us  [on_device(): gates = task_gates.reshape(rows, -1)]
  transfers between devices with their start and end apart: 6 -> 0, of which waited for: 5 -> 0; matrix products, arithmetic and copies ran while one was open for 11% -> 0% of each run, Pallas kernels for 0% -> 0%
where the time goes in v2:
time: 134 us; the launch traced here: 132 us
  Pallas kernels  122 us (91%)
  local copies, waits for them, and re-layouts  7.08 us (5%)
  other arithmetic  2.13 us (2%)
    pallas_call x1, Pallas kernels, on_device(): pl.pallas_call(trunk_kernel, out_shape=(jax.ShapeDtypeStruct((cap, full),...  61.2 us
    pallas_call x1, Pallas kernels, on_device(): pl.pallas_call(expert_kernel, out_shape=(jax.ShapeDtypeStruct((2, rows, w...  61.1 us
    unnamed x8, local copies, waits for them, and re-layouts  5.35 us

profile of v2, /device:TPU:1, one launch (start us, length us, event | category | flops | bytes accessed | tf_op | source)
XLA Modules:
  0.0 132.4 jit_solution(9069083569411224105)
XLA Ops:
  0.6 0.7 reshape.9
  1.3 0.7 convert_reduce_fusion
  2.0 0.2 convolution_convert_fusion
  2.3 0.7 select_reduce_fusion
  3.0 0.7 multiply_add_fusion
  3.7 0.7 broadcast_in_dim.4.gains
  4.4 0.1 copy.28.gates
  4.6 0.1 copy.29.slot_cols
  4.7 0.0 copy-start
  4.7 1.6 %copy-done = bf16[2,2048,256]{2,1,0:T(8,128)(2,1)S(1)} copy-done((bf16[2,2048,256]{2,1,0:T(8,128)(2,1)S(1)}, bf16[2,2048,256]{2,1,0:T(8,128)(2,1)}, u32[]{:S(2)}) %copy-start) | copy-done | bytes 2097176
  6.3 0.0 copy-start.1
  6.3 1.0 copy-done.1
  7.4 0.0 copy-start.2
  7.4 0.9 copy-done.2
  8.3 61.2 %trunk.1 = (bf16[256,2048]{1,0:T(8,128)(2,1)S(1)}, bf16[8,256,256]{2,1,0:T(8,128)(2,1)S(1)}) custom-call(bf16[512,256]{1,0:T(8,128)(2,1)S(1)} %copy-done.2, f32[2,1,2048]{2,1,0:T(1,128)S(1)} %broadcast_in_dim.4.gains, bf16[2,2048,256]{2,1,0:T(8,128)(2,1)S(1)} %copy-done, s32[2,512]{1,0:T(2,128)S(1)} %bitcast.7, f32[512,4]{1,0:T(8,128)S(1)} %copy.28.gates, ...), custom_call_target="tpu_custom_call" | custom-call | flops 6442450944 | bytes 8388608 | tf_op jit(solution)/shard_map/trunk/pallas_call | solution.py:386
  69.5 61.1 %experts.1 = (bf16[2,512,256]{2,1,0:T(8,128)(2,1)S(1)}, f32[128,2048]{1,0:T(8,128)S(1)}) custom-call(bf16[256,2048]{1,0:T(8,128)(2,1)S(1)} %get-tuple-element.6.rows_in, bf16[2048,2048]{1,0:T(8,128)(2,1)} %bitcast.8, bf16[8,256,256]{2,1,0:T(8,128)(2,1)S(1)} %get-tuple-element.7.slot_grad, s32[512,2]{1,0:T(8,128)S(1)} %copy.29.slot_cols, f32[512,4]{1,0:T(8,128)S(1)} %copy.28.gates), custom_call_target="tpu_custom_call" | custom-call | flops 6442450944 | bytes 12582912 | tf_op jit(solution)/shard_map/experts/pallas_call | solution.py:415
  130.7 0.8 copy.33
  131.4 1.0 copy.34
Async XLA Ops:
  4.7 1.6 %copy-start = (bf16[2,2048,256]{2,1,0:T(8,128)(2,1)S(1)}, bf16[2,2048,256]{2,1,0:T(8,128)(2,1)}, u32[]{:S(2)}) copy-start(bf16[2,2048,256]{2,1,0:T(8,128)(2,1)} %weights.1) | copy-start | bytes 6291460
  6.3 1.0 copy-start.1
  7.4 0.9 copy-start.2

commit v3 on v2

v3 whole, which is shorter than its diff:
```python
import math

import jax
import jax.numpy as jnp
from jax import lax
from jax.experimental import pallas as pl
from jax.experimental.pallas import tpu as pltpu
from jax.sharding import PartitionSpec as P

NEMB = 16
DEMB = 128
GROUP = 16
CHUNKS = 4
RELAY = 2
FAR = 1
F32 = jnp.float32
BF16 = jnp.bfloat16
MESH = pl.DeviceIdType.MESH


def dot(a, b):
    return jnp.dot(a, b, preferred_element_type=F32)


def dot_nt(a, b):
    return lax.dot_general(a, b, (((1,), (1,)), ((), ())), preferred_element_type=F32)


def remote(src, dst, send_sem, recv_sem, axis, index):
    return pltpu.make_async_remote_copy(
        src_ref=src, dst_ref=dst, send_sem=send_sem, recv_sem=recv_sem,
        device_id={axis: index}, device_id_type=MESH,
    )


def greet(axis_peers):
    barrier = pltpu.get_barrier_semaphore()
    for axis, peer in axis_peers:
        pl.semaphore_signal(barrier, inc=1, device_id={axis: peer}, device_id_type=MESH)
    pl.semaphore_wait(barrier, len(axis_peers))


def kernel(
    emb, gains, weights, experts_in, ids, gates_in, grad_in, mix_out, wgrad_out,
    whole, nrm, inter, mask, wheld, grad, cot, outg, slot_grad, table, cols,
    held, rows_in, rows_t, slopes, pgrad, outs, ret, first_buf, ring_buf, last_buf,
    lsem, wsem, send, recv, gsend, grecv, send1, recv1, send2, recv2, osend, orecv,
):
    n_dev, cap, width = outs.shape
    rows = emb.shape[0]
    piece, part = first_buf.shape[2:]
    items, live = 3 * CHUNKS, 2 * CHUNKS
    step_rows = rows // CHUNKS
    ring = n_dev // 2
    me = lax.axis_index("tensor")
    dp = lax.axis_index("dp")
    cx, cz = dp // 4, dp % 4
    y, core = me // 2, me % 2
    right = ((y + 1) % ring) * 2 + core
    left = ((y + ring - 1) % ring) * 2 + core
    far = ((y + 2) % ring) * 2 + core
    flip = 1 - 2 * core
    sib = me + flip

    load_emb = pltpu.make_async_copy(emb, whole.at[0, me], lsem.at[0])
    load_grad = pltpu.make_async_copy(grad_in, grad, lsem.at[1])
    load_weights = pltpu.make_async_copy(weights, wheld, lsem.at[2])

    def load_expert(h):
        span = pl.ds(h * 2 * width, 2 * width)
        return pltpu.make_async_copy(experts_in.at[:, span], held.at[:, span], wsem.at[h])

    load_emb.start()
    load_grad.start()
    load_weights.start()

    def copy(i, which):
        turn = (i % 2) * (right - left)
        owner, to = (
            (me, sib), (me, right), (me, left), (left, sib), (right, sib),
            (left + turn, right - turn), (far, sib),
        )[which]
        at = pl.ds((i % CHUNKS) * step_rows, step_rows)
        ref = whole.at[i // CHUNKS, owner, at]
        return remote(ref, ref, send.at[i, which], recv.at[i, which], "tensor", to)

    def arrived(i, which):
        owner = (sib, left, right, left + flip, right + flip, far, far + flip)[which]
        at = pl.ds((i % CHUNKS) * step_rows, step_rows)
        ref = whole.at[i // CHUNKS, owner, at]
        remote(ref, ref, send.at[i, which], recv.at[i, which], "tensor", sib).wait_recv()

    def begin(i):
        for which in (1, 2, 0):
            copy(i, which).start()

    def relay(i):
        arrived(i, 1)
        arrived(i, 2)
        for which in (5, 3, 4):
            copy(i, which).start()

    def relay_far(i):
        arrived(i, 5)
        copy(i, 6).start()

    def complete(i):
        for which in (0, 3, 4, 6):
            arrived(i, which)

    def place(h, u, v):
        return u * 4 + v if h < 2 else v * 4 + u

    coord = [(cx, cz), (cx, cz), (cz, cx), (cz, cx)]
    sign = [1, 3, 1, 3]

    load_emb.wait()
    greet(
        [("tensor", (me + d) % n_dev) for d in range(1, n_dev)]
        + [("dp", place(0, (cx + 1) % 4, cz)), ("dp", place(0, (cx + 3) % 4, cz)),
           ("dp", place(0, cx, (cz + 1) % 4)), ("dp", place(0, cx, (cz + 3) % 4))]
    )

    @pl.loop(0, CHUNKS)
    def _(i):
        begin(i)

    for h in range(4):
        load_expert(h).start()

    row_id = lax.broadcasted_iota(jnp.int32, mask.shape, 0) % GROUP
    col_id = lax.broadcasted_iota(jnp.int32, mask.shape, 1) % GROUP
    mask[...] = jnp.where(row_id == col_id, 1.0 / math.sqrt(DEMB * NEMB), 0.0)

    lane = lax.broadcasted_iota(jnp.int32, (n_dev, rows), 0)
    is_first = (ids[0:1, :] == lane).astype(F32)
    is_second = (ids[1:2, :] == lane).astype(F32)
    member = (is_first + is_second).astype(BF16)
    earlier = (
        lax.broadcasted_iota(jnp.int32, (rows, rows), 0)
        < lax.broadcasted_iota(jnp.int32, (rows, rows), 1)
    ).astype(F32).astype(BF16)
    slot_of = dot(member, earlier) + lane.astype(F32) * cap
    table[...] = jnp.zeros(table.shape, F32)
    table[0:1, :] = jnp.sum(is_first * slot_of, axis=0, keepdims=True)
    table[1:2, :] = jnp.sum(is_second * slot_of, axis=0, keepdims=True)
    for t in range(2):
        table[2 + 2 * t : 4 + 2 * t, :] = gates_in[t]
    cols[...] = table[...].T

    def gate(at, t, k):
        return cols[at, 2 + 2 * t + k : 3 + 2 * t + k]

    def chosen(expert, k):
        wanted = lax.broadcasted_iota(jnp.int32, (cap, rows), 0) + expert * cap
        return (table[k : k + 1, :].astype(jnp.int32) == wanted).astype(F32).astype(BF16)

    load_grad.wait()
    every = slice(0, rows)
    for k in range(2):
        cot[k] = (
            gate(every, 0, k) * grad[0].astype(F32) + gate(every, 1, k) * grad[1].astype(F32)
        ).astype(BF16)

    def cotangent(e):
        outg[e] = (dot(chosen(e, 0), cot[0]) + dot(chosen(e, 1), cot[1])).astype(BF16)

    for e in range(4):
        cotangent(e)
    for i in range(RELAY):
        relay(i)
        if 0 < i <= FAR:
            relay_far(i - 1)
    load_weights.wait()

    @pl.loop(0, live)
    def _(i):
        stage, first = i // CHUNKS, (i % CHUNKS) * step_rows
        span = pl.ds(pl.multiple_of(first, step_rows), step_rows)
        complete(i)

        def tile(n):
            return whole[stage, n // 2, span, (n % 2) * DEMB : (n % 2 + 1) * DEMB].astype(F32)

        total = jnp.zeros((step_rows, DEMB), F32)
        for n in range(NEMB):
            x = tile(n)
            total = total + x * x
        mean = jnp.sum(total, axis=1, keepdims=True) / (NEMB * DEMB)
        scale = lax.rsqrt(mean + 1e-05)
        for n in range(NEMB):
            lanes = slice(n * DEMB, (n + 1) * DEMB)
            gain = jnp.where(stage == 0, gains[0:1, lanes], gains[1:2, lanes])
            nrm[n] = (tile(n) * scale * gain).astype(BF16)
        relay(i + RELAY)
        relay_far(i + FAR)

        @pl.loop(0, step_rows // GROUP // 4)
        def _(g4):
            for g in range(4):
                at = pl.ds(pl.multiple_of((g4 * 4 + g) * GROUP, GROUP), GROUP)
                stack = nrm[:, at, :].reshape(NEMB * GROUP, DEMB)
                gram = dot_nt(stack, stack) * mask[...]
                high = gram.astype(BF16)
                low = (gram - high.astype(F32)).astype(BF16)
                mixed = (dot(high, stack) + dot(low, stack)).astype(BF16)
                mixed = mixed.reshape(NEMB, GROUP, DEMB)
                for n in range(NEMB):
                    inter[at, n * DEMB : (n + 1) * DEMB] = mixed[n]

        pre = dot(inter[...], wheld[stage])
        value = whole[stage, me, span].astype(F32) + pre * jax.nn.sigmoid(pre)
        whole[stage + 1, me, span] = value.astype(BF16)
        begin(i + CHUNKS)

    def to_expert(d):
        to = (me + d) % n_dev
        return remote(outg.at[to], slot_grad.at[me], gsend.at[d], grecv.at[d], "tensor", to)

    for i in range(live, items):
        if i + RELAY < items:
            relay(i + RELAY)
        if i + FAR < items:
            relay_far(i + FAR)
        if i < live + 2:
            for e in range(4 + 2 * (i - live), 6 + 2 * (i - live)):
                cotangent(e)
        if i == items - 1 - FAR:
            @pl.loop(1, n_dev)
            def _(d):
                to_expert(d).start()
        complete(i)
    slot_grad[me] = outg[me]

    mine = (chosen(me, 0).astype(F32) + chosen(me, 1).astype(F32)).astype(BF16)
    for q in range(n_dev):
        rows_in[:, q * width : (q + 1) * width] = dot(mine, whole[2, q]).astype(BF16)
    eye = (
        lax.broadcasted_iota(jnp.int32, (width, width), 0)
        == lax.broadcasted_iota(jnp.int32, (width, width), 1)
    ).astype(F32).astype(BF16)
    for q in range(n_dev):
        rows_t[q * width : (q + 1) * width, :] = dot_nt(
            eye, rows_in[:, q * width : (q + 1) * width]
        ).astype(BF16)

    def partial(h, t, j):
        u, v = coord[h]
        owner = place(h, (u + (4 - sign[h]) * (1 + t)) % 4, (v + (4 - sign[h]) * (1 + j)) % 4)
        at = pl.ds(pl.multiple_of(owner * piece, piece), piece)
        return dot(rows_t[at, :], pgrad[:, h * part : (h + 1) * part])

    def hop1(h, k, src):
        u, v = coord[h]
        return remote(
            src, ring_buf.at[h, k], send1.at[h, k], recv1.at[h, k],
            "dp", place(h, (u + sign[h]) % 4, v),
        )

    def hop2(h, j):
        u, v = coord[h]
        return remote(
            ring_buf.at[h, 8 + j], last_buf.at[h, j],
            send2.at[h, j], recv2.at[h, j], "dp", place(h, u, (v + sign[h]) % 4),
        )

    for p in range(n_dev):
        if p % 2 == 0:
            load_expert(p // 2).wait()
        pre = dot(rows_in[...], held[:, p * width : (p + 1) * width])
        sigma = jax.nn.sigmoid(pre)
        outs[p] = (pre * sigma).astype(BF16)
        slopes[p] = sigma + pre * sigma * (1.0 - sigma)

    @pl.loop(1, n_dev)
    def _(d):
        source = (me + n_dev - d) % n_dev
        remote(
            outg.at[me], slot_grad.at[source], gsend.at[d], grecv.at[d], "tensor", source
        ).wait_recv()

    for h in range(4):
        for p in range(2 * h, 2 * h + 2):
            pgrad[:, p * width : (p + 1) * width] = (
                slot_grad[p].astype(F32) * slopes[p]
            ).astype(BF16)

        @pl.loop(0, 4)
        def _(j):
            first_buf[h, j] = partial(h, 0, j).astype(BF16)
            hop1(h, j, first_buf.at[h, j]).start()

    def out_copy(d):
        to = (me + d) % n_dev
        return remote(outs.at[to], ret.at[me], osend.at[d], orecv.at[d], "tensor", to)

    @pl.loop(1, n_dev)
    def _(d):
        out_copy(d).start()

    ret[me] = outs[me]

    def ring_step(k):
        t, j = k // 4, k % 4
        own = [partial(h, t, j) for h in range(4)]
        for h in range(4):
            hop1(h, k - 4, ring_buf.at[h, k - 4]).wait_recv()
            ring_buf[h, k - 4] = (ring_buf[h, k - 4].astype(F32) + own[h]).astype(BF16)
            hop1(h, k, ring_buf.at[h, k - 4]).start()

    pl.loop(4, 8)(ring_step)

    @pl.loop(1, n_dev)
    def _(d):
        source = (me + n_dev - d) % n_dev
        remote(
            outs.at[me], ret.at[source], osend.at[d], orecv.at[d], "tensor", source
        ).wait_recv()

    block_rows = 128

    @pl.loop(0, rows // block_rows)
    def _(b):
        at = pl.ds(pl.multiple_of(b * block_rows, block_rows), block_rows)
        seat = lax.broadcasted_iota(jnp.int32, (block_rows, cap), 1)
        picked = []
        for k in range(2):
            slot = cols[at, k : k + 1].astype(jnp.int32)
            total = jnp.zeros((block_rows, width), F32)
            for e in range(n_dev):
                hot = (slot == seat + e * cap).astype(F32).astype(BF16)
                total = total + dot(hot, ret[e])
            picked.append(total)
        for t in range(2):
            mix = gate(at, t, 0) * picked[0] + gate(at, t, 1) * picked[1]
            mix_out[t, at, :] = mix.astype(BF16)

    pl.loop(8, 12)(ring_step)

    for j in range(4):
        for h in range(4):
            own = partial(h, 3, j)
            hop1(h, 8 + j, ring_buf.at[h, 8 + j]).wait_recv()
            total = ring_buf[h, 8 + j].astype(F32) + own
            if j > 0:
                hop2(h, j - 1).wait_recv()
                total = total + last_buf[h, j - 1].astype(F32)
            if j < 3:
                ring_buf[h, 8 + j] = total.astype(BF16)
                hop2(h, j).start()
            else:
                wgrad_out[:, h * part : (h + 1) * part] = total

    @pl.loop(0, items)
    def _(i):
        for which in range(7):
            copy(i, which).wait_send()

    for h in range(4):
        @pl.loop(0, 4)
        def _(k):
            hop1(h, k, first_buf.at[h, k]).wait_send()

        @pl.loop(4, 12)
        def _(k):
            hop1(h, k, ring_buf.at[h, k - 4]).wait_send()

        for j in range(3):
            hop2(h, j).wait_send()

    @pl.loop(1, n_dev)
    def _(d):
        to_expert(d).wait_send()
        out_copy(d).wait_send()


VMEM = pl.BlockSpec(memory_space=pltpu.VMEM)
ANY = pl.BlockSpec(memory_space=pl.ANY)
DMA = pltpu.SemaphoreType.DMA


def on_device(
    embeddings, trunk_weights, trunk_gains, expert_weights, route_ids, task_gates, mixture_grad
):
    experts = lax.axis_size("tensor")
    rows, top = route_ids.shape
    cap = 2 * rows * top // experts
    width = embeddings.shape[1]
    full = width * experts
    step_rows = rows // CHUNKS
    piece = full // lax.axis_size("dp")
    by_slot = (experts, cap, width)

    mixture, weight_grad = pl.pallas_call(
        kernel,
        out_shape=(
            jax.ShapeDtypeStruct((2, rows, width), BF16),
            jax.ShapeDtypeStruct((piece, full), F32),
        ),
        in_specs=[ANY, VMEM, ANY, ANY, VMEM, VMEM, ANY],
        out_specs=(VMEM, VMEM),
        scratch_shapes=[
            pltpu.VMEM((3, experts, rows, width), BF16),
            pltpu.VMEM((NEMB, step_rows, DEMB), BF16),
            pltpu.VMEM((step_rows, full), BF16),
            pltpu.VMEM((NEMB * GROUP, NEMB * GROUP), F32),
            pltpu.VMEM((2, full, width), BF16),
            pltpu.VMEM((2, rows, width), BF16),
            pltpu.VMEM((2, rows, width), BF16),
            pltpu.VMEM(by_slot, BF16),
            pltpu.VMEM(by_slot, BF16),
            pltpu.VMEM((128, rows), F32),
            pltpu.VMEM((rows, 128), F32),
            pltpu.VMEM((full, full), BF16),
            pltpu.VMEM((cap, full), BF16),
            pltpu.VMEM((full, cap), BF16),
            pltpu.VMEM(by_slot, F32),
            pltpu.VMEM((cap, full), BF16),
            pltpu.VMEM(by_slot, BF16),
            pltpu.VMEM(by_slot, BF16),
            pltpu.VMEM((4, 4, piece, full // 4), BF16),
            pltpu.VMEM((4, 12, piece, full // 4), BF16),
            pltpu.VMEM((4, 3, piece, full // 4), BF16),
            DMA((3,)),
            DMA((4,)),
            DMA((3 * CHUNKS, 7)),
            DMA((3 * CHUNKS, 7)),
            DMA((experts,)),
            DMA((experts,)),
            DMA((4, 12)),
            DMA((4, 12)),
            DMA((4, 3)),
            DMA((4, 3)),
            DMA((experts,)),
            DMA((experts,)),
        ],
        compiler_params=pltpu.CompilerParams(
            collective_id=0, has_side_effects=True, vmem_limit_bytes=56 << 20
        ),
        cost_estimate=pl.CostEstimate(flops=12 << 30, bytes_accessed=16 << 20, transcendentals=0),
        name="trunk_experts",
    )(
        embeddings, trunk_gains, trunk_weights, expert_weights[0], route_ids.T,
        task_gates.transpose(1, 2, 0), mixture_grad,
    )
    return (mixture, weight_grad[None])


def solution(mesh):
    in_specs = (
        P("dp", "tensor"),
        P(None, None, "tensor"),
        P(),
        P("tensor", None, None),
        P("dp", None),
        P("dp", None, None),
        P(None, "dp", "tensor"),
    )
    out_specs = (P(None, "dp", "tensor"), P("tensor", "dp", None))
    return jax.shard_map(
        on_device, mesh=mesh, in_specs=in_specs, out_specs=out_specs, check_vma=False
    )
```

time: 134 us -> 125 us (0.933); the launches traced: 132 us -> 125 us
  local copies, waits for them, and re-layouts: 7.08 us -> 4.16 us
  other arithmetic: 2.13 us -> 0 us
  Pallas kernels: 122 us -> 120 us
    pallas_call x2 -> x1, Pallas kernels: 122 us -> 120 us  [on_device(): pl.pallas_call(kernel, out_shape=(jax.ShapeDtypeStruct((2, rows, width),...]
    reduce_sum x2 -> x0, other arithmetic: 1.43 us -> none  [the longest x1 0.74 us: slot_table(): place = jnp.sum((route[:, :, None] == lanes) * prefix[:, None, :], axis=2)]
    unnamed x8 -> x2, local copies, waits for them, and re-layouts: 5.35 us -> 4.16 us
where the time goes in v3:
time: 125 us
  Pallas kernels  120 us (96%)
  local copies, waits for them, and re-layouts  4.16 us (3%)
    pallas_call x1, Pallas kernels, on_device(): pl.pallas_call(kernel, out_shape=(jax.ShapeDtypeStruct((2, rows, width),...  120 us
    unnamed x2, local copies, waits for them, and re-layouts  4.16 us

profile of v3, /device:TPU:1, one launch (start us, length us, event | category | flops | bytes accessed | tf_op | source)
XLA Modules:
  0.0 125.2 jit_solution(11708559623153152979)
XLA Ops:
  0.6 120.4 %trunk_experts.1 = (bf16[2,512,256]{2,1,0:T(8,128)(2,1)}, f32[128,2048]{1,0:T(8,128)}) custom-call(bf16[512,256]{1,0:T(8,128)(2,1)} %emb.1, f32[2,2048]{1,0:T(2,128)} %gains.1, bf16[2,2048,256]{2,1,0:T(8,128)(2,1)} %weights.1, bf16[2048,2048]{1,0:T(8,128)(2,1)} %bitcast.5, s32[2,512]{1,0:T(2,128)} %bitcast.7, f32[2,2,512]{2,1,0:T(2,128)} %bitcast.6, ...), custom_call_target="tpu_custom_call" | custom-call | flops 12884901888 | bytes 16777216 | tf_op jit(solution)/shard_map/trunk_experts/pallas_call | solution.py:394
  121.0 1.9 %copy.11 = bf16[2,512,256]{2,1,0:T(8,128)(2,1)} copy(bf16[2,512,256]{2,1,0:T(8,128)(2,1)} %get-tuple-element.8) | data formatting | bytes 1048576
  122.9 2.3 %copy.12 = f32[1,128,2048]{2,1,0:T(8,128)} copy(f32[1,128,2048]{2,1,0:T(8,128)} %bitcast.4) | data formatting | bytes 2097152

commit v4 on v3

--- a/solution.py
+++ b/solution.py
@@ -33,22 +33,15 @@
     )
 
 
-def greet(axis_peers):
-    barrier = pltpu.get_barrier_semaphore()
-    for axis, peer in axis_peers:
-        pl.semaphore_signal(barrier, inc=1, device_id={axis: peer}, device_id_type=MESH)
-    pl.semaphore_wait(barrier, len(axis_peers))
-
-
 def kernel(
-    emb, gains, weights, experts_in, ids, gates_in, grad_in, mix_out, wgrad_out,
-    whole, nrm, inter, mask, wheld, grad, cot, outg, slot_grad, table, cols,
+    emb, gains_in, weights, experts_in, ids_in, gates_in, grad_in, mix_out, wgrad_out,
+    whole, nrm, inter, mask, wheld, grad, gains, ids, gates, cot, outg, slot_grad, table, cols,
     held, rows_in, rows_t, slopes, pgrad, outs, ret, first_buf, ring_buf, last_buf,
-    lsem, wsem, send, recv, gsend, grecv, send1, recv1, send2, recv2, osend, orecv,
+    mix, wgrad, lsem, wsem, send, recv, gsend, grecv, send1, recv1, send2, recv2, osend, orecv, send0, recv0,
 ):
     n_dev, cap, width = outs.shape
     rows = emb.shape[0]
-    piece, part = first_buf.shape[2:]
+    piece, part = last_buf.shape[2:]
     items, live = 3 * CHUNKS, 2 * CHUNKS
     step_rows = rows // CHUNKS
     ring = n_dev // 2
@@ -65,14 +58,28 @@
     load_emb = pltpu.make_async_copy(emb, whole.at[0, me], lsem.at[0])
     load_grad = pltpu.make_async_copy(grad_in, grad, lsem.at[1])
     load_weights = pltpu.make_async_copy(weights, wheld, lsem.at[2])
+    load_gains = pltpu.make_async_copy(gains_in, gains, lsem.at[3])
+    load_ids = pltpu.make_async_copy(ids_in, ids, lsem.at[4])
+    load_gates = pltpu.make_async_copy(gates_in, gates, lsem.at[5])
 
     def load_expert(h):
         span = pl.ds(h * 2 * width, 2 * width)
         return pltpu.make_async_copy(experts_in.at[:, span], held.at[:, span], wsem.at[h])
 
     load_emb.start()
-    load_grad.start()
-    load_weights.start()
+    for load in (load_ids, load_gates, load_gains, load_grad, load_weights):
+        load.start()
+
+    def place(h, u, v):
+        return u * 4 + v if h < 2 else v * 4 + u
+
+    barrier = pltpu.get_barrier_semaphore()
+    peers = [("tensor", (me + d) % n_dev) for d in range(1, n_dev)] + [
+        ("dp", place(0, (cx + 1) % 4, cz)), ("dp", place(0, (cx + 3) % 4, cz)),
+        ("dp", place(0, cx, (cz + 1) % 4)), ("dp", place(0, cx, (cz + 3) % 4)),
+    ]
+    for axis, peer in peers:
+        pl.semaphore_signal(barrier, inc=1, device_id={axis: peer}, device_id_type=MESH)
 
     def copy(i, which):
         turn = (i % 2) * (right - left)
@@ -108,18 +115,11 @@
         for which in (0, 3, 4, 6):
             arrived(i, which)
 
-    def place(h, u, v):
-        return u * 4 + v if h < 2 else v * 4 + u
-
     coord = [(cx, cz), (cx, cz), (cz, cx), (cz, cx)]
     sign = [1, 3, 1, 3]
 
     load_emb.wait()
-    greet(
-        [("tensor", (me + d) % n_dev) for d in range(1, n_dev)]
-        + [("dp", place(0, (cx + 1) % 4, cz)), ("dp", place(0, (cx + 3) % 4, cz)),
-           ("dp", place(0, cx, (cz + 1) % 4)), ("dp", place(0, cx, (cz + 3) % 4))]
-    )
+    pl.semaphore_wait(barrier, len(peers))
 
     @pl.loop(0, CHUNKS)
     def _(i):
@@ -132,6 +132,8 @@
     col_id = lax.broadcasted_iota(jnp.int32, mask.shape, 1) % GROUP
     mask[...] = jnp.where(row_id == col_id, 1.0 / math.sqrt(DEMB * NEMB), 0.0)
 
+    load_ids.wait()
+    load_gates.wait()
     lane = lax.broadcasted_iota(jnp.int32, (n_dev, rows), 0)
     is_first = (ids[0:1, :] == lane).astype(F32)
     is_second = (ids[1:2, :] == lane).astype(F32)
@@ -145,7 +147,7 @@
     table[0:1, :] = jnp.sum(is_first * slot_of, axis=0, keepdims=True)
     table[1:2, :] = jnp.sum(is_second * slot_of, axis=0, keepdims=True)
     for t in range(2):
-        table[2 + 2 * t : 4 + 2 * t, :] = gates_in[t]
+        table[2 + 2 * t : 4 + 2 * t, :] = gates[t]
     cols[...] = table[...].T
 
     def gate(at, t, k):
@@ -171,6 +173,7 @@
         relay(i)
         if 0 < i <= FAR:
             relay_far(i - 1)
+    load_gains.wait()
     load_weights.wait()
 
     @pl.loop(0, live)
@@ -193,10 +196,14 @@
             gain = jnp.where(stage == 0, gains[0:1, lanes], gains[1:2, lanes])
             nrm[n] = (tile(n) * scale * gain).astype(BF16)
         relay(i + RELAY)
-        relay_far(i + FAR)
-
-        @pl.loop(0, step_rows // GROUP // 4)
+        passes = step_rows // GROUP // 4
+
+        @pl.loop(0, passes)
         def _(g4):
+            @pl.when(g4 == passes // 2)
+            def _():
+                relay_far(i + FAR)
+
             for g in range(4):
                 at = pl.ds(pl.multiple_of((g4 * 4 + g) * GROUP, GROUP), GROUP)
                 stack = nrm[:, at, :].reshape(NEMB * GROUP, DEMB)
@@ -220,15 +227,18 @@
     for i in range(live, items):
         if i + RELAY < items:
             relay(i + RELAY)
+            for e in range(4 + 2 * (i - live), 6 + 2 * (i - live)):
+                cotangent(e)
         if i + FAR < items:
             relay_far(i + FAR)
-        if i < live + 2:
-            for e in range(4 + 2 * (i - live), 6 + 2 * (i - live)):
-                cotangent(e)
-        if i == items - 1 - FAR:
-            @pl.loop(1, n_dev)
-            def _(d):
-                to_expert(d).start()
+
+    def send_cotangents():
+        @pl.loop(1, n_dev)
+        def _(d):
+            to_expert(d).start()
+
+    pl.when(core == 0)(send_cotangents)
+    for i in range(live, items):
         complete(i)
     slot_grad[me] = outg[me]
 
@@ -264,31 +274,46 @@
             send2.at[h, j], recv2.at[h, j], "dp", place(h, u, (v + sign[h]) % 4),
         )
 
-    for p in range(n_dev):
-        if p % 2 == 0:
-            load_expert(p // 2).wait()
-        pre = dot(rows_in[...], held[:, p * width : (p + 1) * width])
-        sigma = jax.nn.sigmoid(pre)
-        outs[p] = (pre * sigma).astype(BF16)
-        slopes[p] = sigma + pre * sigma * (1.0 - sigma)
-
-    @pl.loop(1, n_dev)
-    def _(d):
-        source = (me + n_dev - d) % n_dev
-        remote(
-            outg.at[me], slot_grad.at[source], gsend.at[d], grecv.at[d], "tensor", source
-        ).wait_recv()
-
-    for h in range(4):
-        for p in range(2 * h, 2 * h + 2):
-            pgrad[:, p * width : (p + 1) * width] = (
-                slot_grad[p].astype(F32) * slopes[p]
-            ).astype(BF16)
-
-        @pl.loop(0, 4)
-        def _(j):
-            first_buf[h, j] = partial(h, 0, j).astype(BF16)
-            hop1(h, j, first_buf.at[h, j]).start()
+    def hop0(h, j, sub):
+        u, v = coord[h]
+        return remote(
+            first_buf.at[h, sub, j], ring_buf.at[h, j, :, pl.ds(sub * width, width)],
+            send0.at[h, sub, j], recv0.at[h, sub, j], "dp", place(h, (u + sign[h]) % 4, v),
+        )
+
+    for sub in range(2):
+        for p in range(sub, n_dev, 2):
+            if sub == 0:
+                load_expert(p // 2).wait()
+            pre = dot(rows_in[...], held[:, p * width : (p + 1) * width])
+            sigma = jax.nn.sigmoid(pre)
+            outs[p] = (pre * sigma).astype(BF16)
+            slopes[p] = sigma + pre * sigma * (1.0 - sigma)
+        if sub == 0:
+            pl.when(core == 1)(send_cotangents)
+
+        @pl.loop(1, n_dev)
+        def _(d):
+            source = (me + n_dev - d) % n_dev
+
+            @pl.when(source % 2 == sub)
+            def _():
+                remote(
+                    outg.at[me], slot_grad.at[source], gsend.at[d], grecv.at[d], "tensor", source
+                ).wait_recv()
+
+        for h in range(4):
+            p = 2 * h + sub
+            lanes = slice(p * width, (p + 1) * width)
+            pgrad[:, lanes] = (slot_grad[p].astype(F32) * slopes[p]).astype(BF16)
+            u, v = coord[h]
+
+            @pl.loop(0, 4)
+            def _(j):
+                owner = place(h, (u + 4 - sign[h]) % 4, (v + (4 - sign[h]) * (1 + j)) % 4)
+                at = pl.ds(pl.multiple_of(owner * piece, piece), piece)
+                first_buf[h, sub, j] = dot(rows_t[at, :], pgrad[:, lanes]).astype(BF16)
+                hop0(h, j, sub).start()
 
     def out_copy(d):
         to = (me + d) % n_dev
@@ -300,15 +325,21 @@
 
     ret[me] = outs[me]
 
-    def ring_step(k):
+    def ring_step(k, arrive):
         t, j = k // 4, k % 4
         own = [partial(h, t, j) for h in range(4)]
         for h in range(4):
-            hop1(h, k - 4, ring_buf.at[h, k - 4]).wait_recv()
+            arrive(h, k - 4)
             ring_buf[h, k - 4] = (ring_buf[h, k - 4].astype(F32) + own[h]).astype(BF16)
             hop1(h, k, ring_buf.at[h, k - 4]).start()
 
-    pl.loop(4, 8)(ring_step)
+    @pl.loop(4, 8)
+    def _(k):
+        def arrive(h, j):
+            for sub in range(2):
+                hop0(h, j, sub).wait_recv()
+
+        ring_step(k, arrive)
 
     @pl.loop(1, n_dev)
     def _(d):
@@ -332,10 +363,19 @@
                 total = total + dot(hot, ret[e])
             picked.append(total)
         for t in range(2):
-            mix = gate(at, t, 0) * picked[0] + gate(at, t, 1) * picked[1]
-            mix_out[t, at, :] = mix.astype(BF16)
-
-    pl.loop(8, 12)(ring_step)
+            both = gate(at, t, 0) * picked[0] + gate(at, t, 1) * picked[1]
+            mix[t, at, :] = both.astype(BF16)
+
+    store_mix = pltpu.make_async_copy(mix, mix_out, lsem.at[0])
+    store_mix.start()
+
+    def store_wgrad(h):
+        span = pl.ds(h * part, part)
+        return pltpu.make_async_copy(wgrad.at[:, span], wgrad_out.at[:, span], wsem.at[h])
+
+    @pl.loop(8, 12)
+    def _(k):
+        ring_step(k, lambda h, j: hop1(h, j, ring_buf.at[h, j]).wait_recv())
 
     for j in range(4):
         for h in range(4):
@@ -349,7 +389,12 @@
                 ring_buf[h, 8 + j] = total.astype(BF16)
                 hop2(h, j).start()
             else:
-                wgrad_out[:, h * part : (h + 1) * part] = total
+                wgrad[:, h * part : (h + 1) * part] = total
+                store_wgrad(h).start()
+
+    store_mix.wait()
+    for h in range(4):
+        store_wgrad(h).wait()
 
     @pl.loop(0, items)
     def _(i):
@@ -358,8 +403,9 @@
 
     for h in range(4):
         @pl.loop(0, 4)
-        def _(k):
-            hop1(h, k, first_buf.at[h, k]).wait_send()
+        def _(j):
+            for sub in range(2):
+                hop0(h, j, sub).wait_send()
 
         @pl.loop(4, 12)
         def _(k):
@@ -374,8 +420,7 @@
         out_copy(d).wait_send()
 
 
-VMEM = pl.BlockSpec(memory_space=pltpu.VMEM)
-ANY = pl.BlockSpec(memory_space=pl.ANY)
+HBM = pl.BlockSpec(memory_space=pltpu.HBM)
 DMA = pltpu.SemaphoreType.DMA
 
 
@@ -397,8 +442,8 @@
             jax.ShapeDtypeStruct((2, rows, width), BF16),
             jax.ShapeDtypeStruct((piece, full), F32),
         ),
-        in_specs=[ANY, VMEM, ANY, ANY, VMEM, VMEM, ANY],
-        out_specs=(VMEM, VMEM),
+        in_specs=[HBM] * 7,
+        out_specs=(HBM, HBM),
         scratch_shapes=[
             pltpu.VMEM((3, experts, rows, width), BF16),
             pltpu.VMEM((NEMB, step_rows, DEMB), BF16),
@@ -406,6 +451,9 @@
             pltpu.VMEM((NEMB * GROUP, NEMB * GROUP), F32),
             pltpu.VMEM((2, full, width), BF16),
             pltpu.VMEM((2, rows, width), BF16),
+            pltpu.VMEM((2, full), F32),
+            pltpu.VMEM((top, rows), jnp.int32),
+            pltpu.VMEM((2, top, rows), F32),
             pltpu.VMEM((2, rows, width), BF16),
             pltpu.VMEM(by_slot, BF16),
             pltpu.VMEM(by_slot, BF16),
@@ -418,10 +466,12 @@
             pltpu.VMEM((cap, full), BF16),
             pltpu.VMEM(by_slot, BF16),
             pltpu.VMEM(by_slot, BF16),
-            pltpu.VMEM((4, 4, piece, full // 4), BF16),
+            pltpu.VMEM((4, 2, 4, piece, width), BF16),
             pltpu.VMEM((4, 12, piece, full // 4), BF16),
             pltpu.VMEM((4, 3, piece, full // 4), BF16),
-            DMA((3,)),
+            pltpu.VMEM((2, rows, width), BF16),
+            pltpu.VMEM((piece, full), F32),
+            DMA((6,)),
             DMA((4,)),
             DMA((3 * CHUNKS, 7)),
             DMA((3 * CHUNKS, 7)),
@@ -433,6 +483,8 @@
             DMA((4, 3)),
             DMA((experts,)),
             DMA((experts,)),
+            DMA((4, 2, 4)),
+            DMA((4, 2, 4)),
         ],
         compiler_params=pltpu.CompilerParams(
             collective_id=0, has_side_effects=True, vmem_limit_bytes=56 << 20

time: 125 us -> 118 us (0.944)
  Pallas kernels: 120 us -> 113 us
    pallas_call x1, Pallas kernels: 120 us -> 113 us  [on_device(): pl.pallas_call(kernel, out_shape=(jax.ShapeDtypeStruct((2, rows, width),...]
where the time goes in v4:
time: 118 us
  Pallas kernels  113 us (96%)
  local copies, waits for them, and re-layouts  4.16 us (4%)
    pallas_call x1, Pallas kernels, on_device(): pl.pallas_call(kernel, out_shape=(jax.ShapeDtypeStruct((2, rows, width),...  113 us
    unnamed x2, local copies, waits for them, and re-layouts  4.16 us

profile of v4, /device:TPU:1, one launch (start us, length us, event | category | flops | bytes accessed | tf_op | source)
XLA Modules:
  0.0 117.8 jit_solution(2802218173952366915)
XLA Ops:
  0.6 112.9 %trunk_experts.1 = (bf16[2,512,256]{2,1,0:T(8,128)(2,1)}, f32[128,2048]{1,0:T(8,128)}) custom-call(bf16[512,256]{1,0:T(8,128)(2,1)} %emb.1, f32[2,2048]{1,0:T(2,128)} %gains_in.1, bf16[2,2048,256]{2,1,0:T(8,128)(2,1)} %weights.1, bf16[2048,2048]{1,0:T(8,128)(2,1)} %bitcast.5, s32[2,512]{1,0:T(2,128)} %bitcast.7, f32[2,2,512]{2,1,0:T(2,128)} %bitcast.6, ...), custom_call_target="tpu_custom_call" | custom-call | flops 12884901888 | bytes 16777216 | tf_op jit(solution)/shard_map/trunk_experts/pallas_call | solution.py:439
  113.6 1.9 %copy.11 = bf16[2,512,256]{2,1,0:T(8,128)(2,1)} copy(bf16[2,512,256]{2,1,0:T(8,128)(2,1)} %get-tuple-element.8) | data formatting | bytes 1048576
  115.5 2.3 %copy.12 = f32[1,128,2048]{2,1,0:T(8,128)} copy(f32[1,128,2048]{2,1,0:T(8,128)} %bitcast.4) | data formatting | bytes 2097152

commit v5 on v4

--- a/solution.py
+++ b/solution.py
@@ -101,11 +101,18 @@
         for which in (1, 2, 0):
             copy(i, which).start()
 
+        @pl.when(i >= live)
+        def _():
+            at = pl.ds((i % CHUNKS) * step_rows, step_rows)
+            ref = whole.at[i // CHUNKS, me, at]
+            remote(ref, ref, send.at[i, 5], recv.at[i, 5], "tensor", far).start()
+
     def relay(i):
         arrived(i, 1)
         arrived(i, 2)
-        for which in (5, 3, 4):
-            copy(i, which).start()
+        pl.when(i < live)(lambda: copy(i, 5).start())
+        copy(i, 3).start()
+        copy(i, 4).start()
 
     def relay_far(i):
         arrived(i, 5)
@@ -207,10 +214,8 @@
             for g in range(4):
                 at = pl.ds(pl.multiple_of((g4 * 4 + g) * GROUP, GROUP), GROUP)
                 stack = nrm[:, at, :].reshape(NEMB * GROUP, DEMB)
-                gram = dot_nt(stack, stack) * mask[...]
-                high = gram.astype(BF16)
-                low = (gram - high.astype(F32)).astype(BF16)
-                mixed = (dot(high, stack) + dot(low, stack)).astype(BF16)
+                gram = (dot_nt(stack, stack) * mask[...]).astype(BF16)
+                mixed = dot(gram, stack).astype(BF16)
                 mixed = mixed.reshape(NEMB, GROUP, DEMB)
                 for n in range(NEMB):
                     inter[at, n * DEMB : (n + 1) * DEMB] = mixed[n]
@@ -378,10 +383,10 @@
         ring_step(k, lambda h, j: hop1(h, j, ring_buf.at[h, j]).wait_recv())
 
     for j in range(4):
+        own = [partial(h, 3, j) for h in range(4)]
         for h in range(4):
-            own = partial(h, 3, j)
             hop1(h, 8 + j, ring_buf.at[h, 8 + j]).wait_recv()
-            total = ring_buf[h, 8 + j].astype(F32) + own
+            total = ring_buf[h, 8 + j].astype(F32) + own[h]
             if j > 0:
                 hop2(h, j - 1).wait_recv()
                 total = total + last_buf[h, j - 1].astype(F32)

time: 118 us -> 115 us (0.975)
  Pallas kernels: 113 us -> 110 us
    pallas_call x1, Pallas kernels: 113 us -> 110 us  [on_device(): pl.pallas_call(kernel, out_shape=(jax.ShapeDtypeStruct((2, rows, width),...]
where the time goes in v5:
time: 115 us
  Pallas kernels  110 us (96%)
  local copies, waits for them, and re-layouts  4.16 us (4%)
    pallas_call x1, Pallas kernels, on_device(): pl.pallas_call(kernel, out_shape=(jax.ShapeDtypeStruct((2, rows, width),...  110 us
    unnamed x2, local copies, waits for them, and re-layouts  4.16 us

profile of v5, /device:TPU:1, one launch (start us, length us, event | category | flops | bytes accessed | tf_op | source)
XLA Modules:
  0.0 115.1 jit_solution(13687843144574452703)
XLA Ops:
  0.6 110.3 %trunk_experts.1 = (bf16[2,512,256]{2,1,0:T(8,128)(2,1)}, f32[128,2048]{1,0:T(8,128)}) custom-call(bf16[512,256]{1,0:T(8,128)(2,1)} %emb.1, f32[2,2048]{1,0:T(2,128)} %gains_in.1, bf16[2,2048,256]{2,1,0:T(8,128)(2,1)} %weights.1, bf16[2048,2048]{1,0:T(8,128)(2,1)} %bitcast.5, s32[2,512]{1,0:T(2,128)} %bitcast.7, f32[2,2,512]{2,1,0:T(2,128)} %bitcast.6, ...), custom_call_target="tpu_custom_call" | custom-call | flops 12884901888 | bytes 16777216 | tf_op jit(solution)/shard_map/trunk_experts/pallas_call | solution.py:444
  110.9 1.9 %copy.11 = bf16[2,512,256]{2,1,0:T(8,128)(2,1)} copy(bf16[2,512,256]{2,1,0:T(8,128)(2,1)} %get-tuple-element.8) | data formatting | bytes 1048576
  112.8 2.3 %copy.12 = f32[1,128,2048]{2,1,0:T(8,128)} copy(f32[1,128,2048]{2,1,0:T(8,128)} %bitcast.4) | data formatting | bytes 2097152

commit v6 on v5

--- a/solution.py
+++ b/solution.py
@@ -98,14 +98,14 @@
         remote(ref, ref, send.at[i, which], recv.at[i, which], "tensor", sib).wait_recv()
 
     def begin(i):
-        for which in (1, 2, 0):
-            copy(i, which).start()
-
         @pl.when(i >= live)
         def _():
             at = pl.ds((i % CHUNKS) * step_rows, step_rows)
             ref = whole.at[i // CHUNKS, me, at]
             remote(ref, ref, send.at[i, 5], recv.at[i, 5], "tensor", far).start()
+
+        for which in (1, 2, 0):
+            copy(i, which).start()
 
     def relay(i):
         arrived(i, 1)

time: 115 us -> 115 us (level)
  no operation moved by 1% of the time
where the time goes in v6:
time: 115 us
  Pallas kernels  110 us (96%)
  local copies, waits for them, and re-layouts  4.16 us (4%)
    pallas_call x1, Pallas kernels, on_device(): pl.pallas_call(kernel, out_shape=(jax.ShapeDtypeStruct((2, rows, width),...  110 us
    unnamed x2, local copies, waits for them, and re-layouts  4.16 us

profile of v6, /device:TPU:1, one launch (start us, length us, event | category | flops | bytes accessed | tf_op | source)
XLA Modules:
  0.0 115.3 jit_solution(10485887021686965259)
XLA Ops:
  0.6 110.5 %trunk_experts.1 = (bf16[2,512,256]{2,1,0:T(8,128)(2,1)}, f32[128,2048]{1,0:T(8,128)}) custom-call(bf16[512,256]{1,0:T(8,128)(2,1)} %emb.1, f32[2,2048]{1,0:T(2,128)} %gains_in.1, bf16[2,2048,256]{2,1,0:T(8,128)(2,1)} %weights.1, bf16[2048,2048]{1,0:T(8,128)(2,1)} %bitcast.5, s32[2,512]{1,0:T(2,128)} %bitcast.7, f32[2,2,512]{2,1,0:T(2,128)} %bitcast.6, ...), custom_call_target="tpu_custom_call" | custom-call | flops 12884901888 | bytes 16777216 | tf_op jit(solution)/shard_map/trunk_experts/pallas_call | solution.py:444
  111.1 1.9 %copy.11 = bf16[2,512,256]{2,1,0:T(8,128)(2,1)} copy(bf16[2,512,256]{2,1,0:T(8,128)(2,1)} %get-tuple-element.8) | data formatting | bytes 1048576
  113.0 2.3 %copy.12 = f32[1,128,2048]{2,1,0:T(8,128)} copy(f32[1,128,2048]{2,1,0:T(8,128)} %bitcast.4) | data formatting | bytes 2097152

commit v7 on v5

--- a/solution.py
+++ b/solution.py
@@ -164,6 +164,7 @@
         wanted = lax.broadcasted_iota(jnp.int32, (cap, rows), 0) + expert * cap
         return (table[k : k + 1, :].astype(jnp.int32) == wanted).astype(F32).astype(BF16)
 
+    relay(0)
     load_grad.wait()
     every = slice(0, rows)
     for k in range(2):
@@ -174,12 +175,12 @@
     def cotangent(e):
         outg[e] = (dot(chosen(e, 0), cot[0]) + dot(chosen(e, 1), cot[1])).astype(BF16)
 
+    for i in range(1, RELAY):
+        relay(i)
     for e in range(4):
         cotangent(e)
-    for i in range(RELAY):
-        relay(i)
-        if 0 < i <= FAR:
-            relay_far(i - 1)
+    for i in range(FAR):
+        relay_far(i)
     load_gains.wait()
     load_weights.wait()
 
@@ -203,22 +204,17 @@
             gain = jnp.where(stage == 0, gains[0:1, lanes], gains[1:2, lanes])
             nrm[n] = (tile(n) * scale * gain).astype(BF16)
         relay(i + RELAY)
-        passes = step_rows // GROUP // 4
-
-        @pl.loop(0, passes)
-        def _(g4):
-            @pl.when(g4 == passes // 2)
-            def _():
+        groups = step_rows // GROUP
+        for g in range(groups):
+            if g == groups // 2:
                 relay_far(i + FAR)
-
-            for g in range(4):
-                at = pl.ds(pl.multiple_of((g4 * 4 + g) * GROUP, GROUP), GROUP)
-                stack = nrm[:, at, :].reshape(NEMB * GROUP, DEMB)
-                gram = (dot_nt(stack, stack) * mask[...]).astype(BF16)
-                mixed = dot(gram, stack).astype(BF16)
-                mixed = mixed.reshape(NEMB, GROUP, DEMB)
-                for n in range(NEMB):
-                    inter[at, n * DEMB : (n + 1) * DEMB] = mixed[n]
+            at = slice(g * GROUP, (g + 1) * GROUP)
+            stack = nrm[:, at, :].reshape(NEMB * GROUP, DEMB)
+            gram = (dot_nt(stack, stack) * mask[...]).astype(BF16)
+            mixed = dot(gram, stack).astype(BF16)
+            mixed = mixed.reshape(NEMB, GROUP, DEMB)
+            for n in range(NEMB):
+                inter[at, n * DEMB : (n + 1) * DEMB] = mixed[n]
 
         pre = dot(inter[...], wheld[stage])
         value = whole[stage, me, span].astype(F32) + pre * jax.nn.sigmoid(pre)

time: 115 us -> 115 us (level)
  no operation moved by 1% of the time
where the time goes in v7:
time: 115 us
  Pallas kernels  110 us (96%)
  local copies, waits for them, and re-layouts  4.16 us (4%)
    pallas_call x1, Pallas kernels, on_device(): pl.pallas_call(kernel, out_shape=(jax.ShapeDtypeStruct((2, rows, width),...  110 us
    unnamed x2, local copies, waits for them, and re-layouts  4.16 us

profile of v7, /device:TPU:1, one launch (start us, length us, event | category | flops | bytes accessed | tf_op | source)
XLA Modules:
  0.0 115.1 jit_solution(16126635250458982604)
XLA Ops:
  0.6 110.3 %trunk_experts.1 = (bf16[2,512,256]{2,1,0:T(8,128)(2,1)}, f32[128,2048]{1,0:T(8,128)}) custom-call(bf16[512,256]{1,0:T(8,128)(2,1)} %emb.1, f32[2,2048]{1,0:T(2,128)} %gains_in.1, bf16[2,2048,256]{2,1,0:T(8,128)(2,1)} %weights.1, bf16[2048,2048]{1,0:T(8,128)(2,1)} %bitcast.5, s32[2,512]{1,0:T(2,128)} %bitcast.7, f32[2,2,512]{2,1,0:T(2,128)} %bitcast.6, ...), custom_call_target="tpu_custom_call" | custom-call | flops 12884901888 | bytes 16777216 | tf_op jit(solution)/shard_map/trunk_experts/pallas_call | solution.py:440
  110.9 1.9 %copy.11 = bf16[2,512,256]{2,1,0:T(8,128)(2,1)} copy(bf16[2,512,256]{2,1,0:T(8,128)(2,1)} %get-tuple-element.8) | data formatting | bytes 1048576
  112.8 2.3 %copy.12 = f32[1,128,2048]{2,1,0:T(8,128)} copy(f32[1,128,2048]{2,1,0:T(8,128)} %bitcast.4) | data formatting | bytes 2097152
